TPU v7x, 512 devices: a whole 4x4x16 slice. The times are simulated.
512 devices in a mesh: grp: 32 (over x, y, core), dev: 16 (over z).
Axes of the slice: x: 4, y: 4, z: 16, core: 2. Of those that a mesh axis runs over, the one named last changes fastest.
Arguments:
- embeddings: bfloat16 [262144, 768], P(('grp', 'dev')), may hold values from -64 to 64
- codeword_ids: int32 [262144, 96], P(('grp', 'dev')), may hold values from 0 to 255
Outputs:
- rotation: float32 [768, 768], P('dev')
- codebooks: float32 [96, 8, 256], replicated
All inputs are finite; a program needn't handle non-finite values.
Results may differ from a plain program's by a relative error of at most 0.00065.
The roundings to bfloat16 on the way count: a program that leaves them out, or rounds other values in their place, can miss the bound.
Values may be sent and summed in bfloat16 or wider, within the bound.
A program may use at most 64 MiB of HBM per device.

v0:
```python
import jax
import jax.numpy as jnp
from jax import lax
from jax.sharding import PartitionSpec as P

K = 256
NS_STEPS = 5


def onehot_rows(ids_group):
    return (ids_group[:, :, None] == jnp.arange(K, dtype=jnp.int32)[None, None, :]).astype(
        jnp.bfloat16
    )


def group_layout(field, groups):
    rows_local = field.shape[0]
    return field.reshape(rows_local, groups, field.shape[1] // groups).transpose(1, 0, 2)


def group_sums(field, grouped_ids, sub_width, want_counts):
    rows_local = field.shape[0]
    groups = grouped_ids.shape[0]

    def per_group(members):
        ids_group, field_group = members
        selector = onehot_rows(ids_group)
        values = field_group.reshape(rows_local, 8, sub_width)
        totals = jnp.einsum("rmj,rmk->mjk", values, selector, preferred_element_type=jnp.float32)
        if want_counts:
            return (totals, jnp.sum(selector, axis=0, dtype=jnp.float32))
        return totals

    outcome = lax.map(per_group, (grouped_ids, group_layout(field, groups)))
    if want_counts:
        return (outcome[0].reshape(groups * 8, sub_width, K), outcome[1].reshape(groups * 8, K))
    return outcome.reshape(groups * 8, sub_width, K)


def on_device(embeddings, codeword_ids):
    rows_local, width = embeddings.shape
    subspaces = codeword_ids.shape[1]
    sub_width = width // subspaces
    groups = subspaces // 8
    grouped_ids = codeword_ids.reshape(rows_local, groups, 8).transpose(1, 0, 2)
    code_totals, code_counts = group_sums(embeddings, grouped_ids, sub_width, True)
    code_totals, code_counts = lax.psum((code_totals, code_counts), ("grp", "dev"))
    divisor = code_counts[:, None, :] + 1.0
    first_books = (code_totals / divisor).astype(jnp.bfloat16)

    def rebuild(members):
        ids_group, books_group = members
        selector = onehot_rows(ids_group)
        rebuilt = jnp.einsum(
            "rmk,mjk->rmj", selector, books_group, preferred_element_type=jnp.float32
        )
        return rebuilt.astype(jnp.bfloat16).reshape(rows_local, 8 * sub_width)

    recon_groups = lax.map(rebuild, (grouped_ids, first_books.reshape(groups, 8, sub_width, K)))
    recon = recon_groups.transpose(1, 0, 2).reshape(rows_local, width)
    partial_cross = lax.dot_general(
        embeddings, recon, (((0,), (0,)), ((), ())), preferred_element_type=jnp.float32
    )
    share = width // lax.axis_size("dev")
    cross_full = lax.psum(partial_cross, ("grp", "dev"))
    cross_own = lax.dynamic_slice_in_dim(cross_full, lax.axis_index("dev") * share, share, 0)
    scale = 2.0 * jnp.sqrt((jnp.sum(cross_full * cross_full) + 1e-06) / width)
    current_full = cross_full / scale
    current_rows = cross_own / scale
    for step_no in range(NS_STEPS):
        if step_no > 0:
            current_full = lax.all_gather(current_rows, "dev", axis=0, tiled=True)
        inner = jnp.dot(
            current_rows,
            current_full.T,
            precision=lax.Precision.HIGHEST,
            preferred_element_type=jnp.float32,
        )
        cubic = jnp.dot(
            inner, current_full, precision=lax.Precision.HIGHEST, preferred_element_type=jnp.float32
        )
        current_rows = 1.5 * current_rows - 0.5 * cubic
    rotation_full = lax.all_gather(current_rows.astype(jnp.bfloat16), "dev", axis=0, tiled=True)
    rotated = jnp.dot(embeddings, rotation_full, preferred_element_type=jnp.float32).astype(
        jnp.bfloat16
    )
    rotated_totals = group_sums(rotated, grouped_ids, sub_width, False)
    rotated_totals = lax.psum(rotated_totals, ("grp", "dev"))
    return (current_rows, rotated_totals / divisor)


def solution(mesh):
    return jax.shard_map(
        on_device,
        mesh=mesh,
        in_specs=(P(("grp", "dev"), None), P(("grp", "dev"), None)),
        out_specs=(P("dev", None), P()),
        check_vma=False,
    )
```

profile of v0, /device:TPU:1, one launch (start us, length us, event | category | flops | bytes accessed | tf_op | source)
XLA Modules:
  0.0 1910.5 jit_solution(10250049320893804602)
XLA Ops:
  7.2 1.4 copy.23
  8.7 41.0 %while.32 = (s32[]{:T(128)}, f32[12,8,8,256]{3,2,1,0:T(8,128)S(1)}, f32[12,8,256]{2,1,0:T(8,128)}, bf16[12,512,64]{1,2,0:T(8,128)(2,1)S(1)}, s32[12,512,8]{1,2,0:T(8,128)}, /*index=5*/s32[]{:T(128)}) while((s32[]{:T(128)}, f32[12,8,8,256]{3,2,1,0:T(8,128)S(1)}, f32[12,8,256]{2,1,0:T(8,128)}, bf16[12,512,64]{1,2,0:T(8,128)(2,1)S(1)}, ...), condition=%wide.region_2.3_spmd, body=%wide.region_0.2_spmd.sunk | while | flops 22018048 | bytes 222793 | solution.py:34
  9.4 1.4 fusion.63
  12.9 1.4 fusion.63
  16.3 1.4 fusion.63
  19.7 1.4 fusion.63
  23.1 1.4 fusion.63
  26.5 1.4 fusion.63
  29.9 1.4 fusion.63
  33.3 1.4 fusion.63
  36.8 1.4 fusion.63
  40.2 1.4 fusion.63
  43.6 1.4 fusion.63
  47.0 1.4 fusion.63
  50.7 467.2 %all-reduce.9.cloned.1.call-done = (f32[96,8,256]{2,1,0:T(8,128)}, f32[96,256]{1,0:T(8,128)}) async-done(((f32[96,8,256]{2,1,0:T(8,128)}, f32[96,256]{1,0:T(8,128)}), (f32[96,8,256]{2,1,0:T(8,128)}, f32[96,256]{1,0:T(8,128)})) %all-reduce.9.cloned.1.call-update) | async-done | bytes 884752 | tf_op jit(solution)/shard_map/psum | solution.py:47
  520.0 20.7 %while.33 = (s32[]{:T(128)}, bf16[12,512,64]{1,2,0:T(8,128)(2,1)S(1)}, bf16[12,8,8,256]{3,2,1,0:T(8,128)(2,1)S(1)}, s32[12,512,8]{1,2,0:T(8,128)}, s32[]{:T(128)}) while((s32[]{:T(128)}, bf16[12,512,64]{1,2,0:T(8,128)(2,1)S(1)}, bf16[12,8,8,256]{3,2,1,0:T(8,128)(2,1)S(1)}, s32[12,512,8]{1,2,0:T(8,128)}, s32[]{:T(128)}) %tuple.80), condition=%wide.region_6.7_spmd, body=%wide.region_5.6_spmd.sunk | while | flops 17858560 | bytes 148545 | solution.py:59
  540.7 2.3 convolution_bitcast_fusion
  543.0 477.2 %all-reduce.5.cloned.1.call-done = f32[768,768]{1,0:T(8,128)} async-done(((f32[768,768]{1,0:T(8,128)}), f32[768,768]{1,0:T(8,128)}) %all-reduce.5.cloned.1.call-update) | async-done | bytes 2359312 | tf_op jit(solution)/shard_map/psum | solution.py:65
  1020.3 3.0 multiply_reduce_fusion
  1024.0 2.2 fusion.28
  1026.2 2.2 fusion.27
  1028.5 64.5 %all-gather.6.cloned.1.call-done = f32[768,768]{1,0:T(8,128)} async-done(((f32[48,768]{1,0:T(8,128)}), f32[768,768]{1,0:T(8,128)}) %all-gather.6.cloned.1.call-update) | async-done | bytes 2359312 | tf_op jit(solution)/shard_map/all_gather | solution.py:72
  1093.1 4.2 fusion.31
  1097.2 2.2 fusion.26
  1099.7 70.9 %all-gather.8.cloned.1.call-done = f32[768,768]{1,0:T(8,128)} async-done(((f32[48,768]{1,0:T(8,128)}), f32[768,768]{1,0:T(8,128)}) %all-gather.8.cloned.1.call-update) | async-done | bytes 2359312 | tf_op jit(solution)/shard_map/all_gather | solution.py:72
  1170.5 4.2 fusion.32
  1174.7 2.2 fusion.25
  1176.9 71.0 %all-gather.10.cloned.1.call-done = f32[768,768]{1,0:T(8,128)} async-done(((f32[48,768]{1,0:T(8,128)}), f32[768,768]{1,0:T(8,128)}) %all-gather.10.cloned.1.call-update) | async-done | bytes 2359312 | tf_op jit(solution)/shard_map/all_gather | solution.py:72
  1248.0 4.2 fusion.33
  1252.2 2.2 fusion.24
  1254.4 71.0 %all-gather.12.cloned.1.call-done = f32[768,768]{1,0:T(8,128)} async-done(((f32[48,768]{1,0:T(8,128)}), f32[768,768]{1,0:T(8,128)}) %all-gather.12.cloned.1.call-update) | async-done | bytes 2359312 | tf_op jit(solution)/shard_map/all_gather | solution.py:72
  1325.4 4.2 fusion.34
  1329.6 2.2 fusion.30
  1331.9 67.9 %all-gather.14.cloned.1.call-done = bf16[768,768]{1,0:T(8,128)(2,1)} async-done(((bf16[48,768]{1,0:T(8,128)(2,1)}), bf16[768,768]{1,0:T(8,128)(2,1)}) %all-gather.14.cloned.1.call-update) | async-done | bytes 1179664 | tf_op jit(solution)/shard_map/all_gather | solution.py:83
  1399.7 2.1 convolution_convert_fusion
  1401.9 25.0 %while.34 = (s32[]{:T(128)}, f32[12,8,8,256]{3,2,1,0:T(8,128)S(1)}, bf16[12,512,64]{1,2,0:T(8,128)(2,1)S(1)}, s32[12,512,8]{1,2,0:T(8,128)}, s32[]{:T(128)}) while((s32[]{:T(128)}, f32[12,8,8,256]{3,2,1,0:T(8,128)S(1)}, bf16[12,512,64]{1,2,0:T(8,128)(2,1)S(1)}, s32[12,512,8]{1,2,0:T(8,128)}, s32[]{:T(128)}) %tuple.82), condition=%wide.region_10.11_spmd, body=%wide.region_9.10_spmd.sunk | while | flops 17825792 | bytes 181313 | solution.py:34
  1402.6 1.4 fusion.67
  1404.7 1.4 fusion.67
  1406.8 1.4 fusion.67
  1408.9 1.4 fusion.67
  1411.0 1.4 fusion.67
  1413.0 1.4 fusion.67
  1415.1 1.4 fusion.67
  1417.2 1.4 fusion.67
  1421.4 1.4 fusion.67
  1425.5 1.4 fusion.67
  1427.8 473.8 %all-reduce.7.cloned.1.call-done = f32[96,8,256]{2,1,0:T(8,128)} async-done(((f32[96,8,256]{2,1,0:T(8,128)}), f32[96,8,256]{2,1,0:T(8,128)}) %all-reduce.7.cloned.1.call-update) | async-done | bytes 786448 | tf_op jit(solution)/shard_map/psum | solution.py:88
  1901.6 2.1 broadcast_divide_fusion.3
  (120 shorter events, 61.4 us)
Async XLA Ops:
  7.2 510.7 %all-reduce.9.cloned.1.call-start = ((), (), s32[]{:S(2)}) async-start(), calls=%async_computation.7 | async-start | bytes 1769472 | tf_op jit(solution)/shard_map/psum | solution.py:47
  49.7 0.9 copy-start.4
  50.6 969.7 %all-reduce.5.cloned.1.call-start = ((), (), s32[]{:S(2)}) async-start(), calls=%async_computation | async-start | bytes 4718592 | tf_op jit(solution)/shard_map/psum | solution.py:65
  520.0 20.7 %copy-start.6 = (bf16[512,768]{1,0:T(8,128)(2,1)S(1)}, bf16[512,768]{1,0:T(8,128)(2,1)}, u32[]{:S(2)}) copy-start(bf16[512,768]{1,0:T(8,128)(2,1)} %param.8) | copy-start | bytes 2359300
  543.0 550.1 %all-gather.6.cloned.1.call-start = ((), (), s32[]{:S(2)}) async-start(), calls=%async_computation.1 | async-start | bytes 2506752 | tf_op jit(solution)/shard_map/all_gather | solution.py:72
  1020.3 3.7 copy-start.7
  1028.5 68.7 %copy-start.11 = (f32[48,768]{1,0:T(8,128)S(1)}, f32[48,768]{1,0:T(8,128)}, u32[]{:S(2)}) copy-start(f32[48,768]{1,0:T(8,128)} %fusion.27) | copy-start | bytes 442372
  1028.5 142.0 %all-gather.8.cloned.1.call-start = ((), (), s32[]{:S(2)}) async-start(), calls=%async_computation.2 | async-start | bytes 2506752 | tf_op jit(solution)/shard_map/all_gather | solution.py:72
  1093.1 4.2 copy-start.1
  1099.4 75.3 %copy-start.9 = (f32[48,768]{1,0:T(8,128)S(1)}, f32[48,768]{1,0:T(8,128)}, u32[]{:S(2)}) copy-start(f32[48,768]{1,0:T(8,128)} %fusion.26) | copy-start | bytes 442372
  1099.4 148.5 %all-gather.10.cloned.1.call-start = ((), (), s32[]{:S(2)}) async-start(), calls=%async_computation.3 | async-start | bytes 2506752 | tf_op jit(solution)/shard_map/all_gather | solution.py:72
  1170.5 4.2 copy-start.2
  1176.9 75.3 %copy-start.10 = (f32[48,768]{1,0:T(8,128)S(1)}, f32[48,768]{1,0:T(8,128)}, u32[]{:S(2)}) copy-start(f32[48,768]{1,0:T(8,128)} %fusion.25) | copy-start | bytes 442372
  1176.9 148.5 %all-gather.12.cloned.1.call-start = ((), (), s32[]{:S(2)}) async-start(), calls=%async_computation.4 | async-start | bytes 2506752 | tf_op jit(solution)/shard_map/all_gather | solution.py:72
  1248.0 4.2 copy-start.3
  1254.3 75.3 %copy-start.8 = (f32[48,768]{1,0:T(8,128)S(1)}, f32[48,768]{1,0:T(8,128)}, u32[]{:S(2)}) copy-start(f32[48,768]{1,0:T(8,128)} %fusion.24) | copy-start | bytes 442372
  1254.3 145.4 %all-gather.14.cloned.1.call-start = ((), (), s32[]{:S(2)}) async-start(), calls=%async_computation.5 | async-start | bytes 1253376 | tf_op jit(solution)/shard_map/all_gather | solution.py:83
  1325.4 4.2 copy-start
  1331.8 569.7 %all-reduce.7.cloned.1.call-start = ((), (), s32[]{:S(2)}) async-start(), calls=%async_computation.6 | async-start | bytes 1572864 | tf_op jit(solution)/shard_map/psum | solution.py:88
  1426.9 0.9 copy-start.5
Sparse Core Ops, SparseCore 0:
  50.7 467.0 all-reduce.8
  543.1 477.1 all-reduce.4
  1028.6 64.3 all-gather.5
  1099.5 70.9 all-gather.7
  1177.0 70.9 all-gather.9
  1254.5 70.9 all-gather.11
  1331.9 67.7 all-gather.13
  1427.9 473.5 all-reduce.6
where the time goes:
time: 1910 us
  waiting for transfers between devices  1760 us (92%)
  matrix products  78.5 us (4%)
  local copies, waits for them, and re-layouts  36.7 us (2%)
    psum x1, waiting for transfers between devices, on_device(): cross_full = lax.psum(partial_cross, ('grp', 'dev'))  477 us
    psum x1, waiting for transfers between devices, on_device(): rotated_totals = lax.psum(rotated_totals, ('grp', 'dev'))  474 us
    psum x1, waiting for transfers between devices, on_device(): lax.psum((code_totals, code_counts), ('grp', 'dev'))  467 us
    all_gather x4, waiting for transfers between devices, on_device(): current_full = lax.all_gather(current_rows, 'dev', axis=0, tiled=True)  277 us
    all_gather x1, waiting for transfers between devices, on_device(): lax.all_gather(current_rows.astype(jnp.bfloat16), 'dev', axis=0, tiled=True)  67.9 us
  transfers between devices with their start and end apart: 8, of which 8 were waited for; matrix products, arithmetic and copies ran while one was open for 0% of the time, Pallas kernels for 0%

commit v1 on v0

--- a/solution.py
+++ b/solution.py
@@ -1,10 +1,269 @@
+import functools
+
 import jax
 import jax.numpy as jnp
 from jax import lax
+from jax.experimental import pallas as pl
+from jax.experimental.pallas import tpu as pltpu
 from jax.sharding import PartitionSpec as P
 
 K = 256
 NS_STEPS = 5
+LANES = 128
+MESH = pl.DeviceIdType.MESH
+TORUS = (4, 4)
+
+
+def all_sum_kernel(
+    nx, ny, nz, x_ref, out_ref,
+    pair_buf, plane_buf, acc, z_src, z_buf, z_all,
+    pair_sem, plane_sem, line_sem, line_back_sem, plane_back_sem, pair_back_sem, send_sem,
+):
+    planes = nx * ny
+    rows, cols = x_ref.shape
+    half, part = rows // 2, rows // (2 * planes)
+    lane_tiles = cols // LANES
+    per_z = part * lane_tiles // nz
+    grp, z = lax.axis_index("grp"), lax.axis_index("dev")
+    core, xy = lax.rem(grp, 2), lax.div(grp, 2)
+    x, y = lax.div(xy, ny), lax.rem(xy, ny)
+
+    def ahead(i):
+        return lax.rem(x + lax.div(i, ny), nx) * ny + lax.rem(y + lax.rem(i, ny), ny)
+
+    def behind(i):
+        return lax.rem(x + nx - lax.div(i, ny), nx) * ny + lax.rem(y + ny - lax.rem(i, ny), ny)
+
+    def sibling():
+        return {"grp": xy * 2 + 1 - core, "dev": z}
+
+    def in_plane(g):
+        return {"grp": g * 2 + core, "dev": z}
+
+    def in_line(i):
+        return {"grp": grp, "dev": lax.rem(z + i, nz)}
+
+    def chunk(which_core, g):
+        return pl.ds(pl.multiple_of(which_core * half + g * part, 8), part)
+
+    def piece(g):
+        return pl.ds(pl.multiple_of(g * part, 8), part)
+
+    def copy(src, dst, send, recv, device):
+        return pltpu.make_async_remote_copy(
+            src_ref=src, dst_ref=dst, send_sem=send, recv_sem=recv,
+            device_id=device, device_id_type=MESH,
+        )
+
+    barrier = pltpu.get_barrier_semaphore()
+    pl.semaphore_signal(barrier, inc=1, device_id=sibling(), device_id_type=MESH)
+
+    @pl.loop(1, planes)
+    def _(i):
+        pl.semaphore_signal(barrier, inc=1, device_id=in_plane(ahead(i)), device_id_type=MESH)
+
+    @pl.loop(1, nz)
+    def _(i):
+        pl.semaphore_signal(barrier, inc=1, device_id=in_line(i), device_id_type=MESH)
+
+    pl.semaphore_wait(barrier, 1 + planes - 1 + nz - 1)
+
+    def pair_copy(i):
+        g = ahead(lax.rem(i, planes))
+        return copy(
+            x_ref.at[chunk(1 - core, g)], pair_buf.at[piece(g)],
+            send_sem.at[0], pair_sem.at[lax.rem(i, planes)], sibling(),
+        )
+
+    @pl.loop(1, planes + 1)
+    def _(i):
+        pair_copy(i).start()
+
+    def plane_copy(i):
+        g = ahead(i)
+        return copy(
+            pair_buf.at[piece(g)], plane_buf.at[i - 1],
+            send_sem.at[1], plane_sem.at[i - 1], in_plane(g),
+        )
+
+    @pl.loop(1, planes)
+    def _(i):
+        pair_copy(i).wait_recv()
+        g = ahead(i)
+        pair_buf[piece(g)] = pair_buf[piece(g)] + x_ref[chunk(core, g)]
+        plane_copy(i).start()
+
+    pair_copy(planes).wait_recv()
+    acc[...] = pair_buf[piece(xy)] + x_ref[chunk(core, xy)]
+
+    @pl.loop(1, planes)
+    def _(i):
+        plane_copy(i).wait_recv()
+        acc[...] += plane_buf[i - 1]
+
+    for s in range(part):
+        for l in range(lane_tiles):
+            r = s * lane_tiles + l
+            z_src[r // per_z, r % per_z] = acc[s : s + 1, l * LANES : (l + 1) * LANES]
+
+    def line_copy(i):
+        return copy(
+            z_src.at[lax.rem(z + i, nz)], z_buf.at[i - 1],
+            send_sem.at[2], line_sem.at[i - 1], in_line(i),
+        )
+
+    def line_back_copy(i):
+        return copy(
+            z_all.at[z], z_all.at[z], send_sem.at[3], line_back_sem.at[i - 1], in_line(i),
+        )
+
+    @pl.loop(1, nz)
+    def _(i):
+        line_copy(i).start()
+
+    z_all[z] = z_src[z]
+
+    @pl.loop(1, nz)
+    def _(i):
+        line_copy(i).wait_recv()
+        z_all[z] += z_buf[i - 1]
+
+    @pl.loop(1, nz)
+    def _(i):
+        line_back_copy(i).start()
+
+    def line_back_arrival(i):
+        landed = z_all.at[lax.rem(z + nz - i, nz)]
+        return copy(landed, landed, send_sem.at[3], line_back_sem.at[i - 1], in_line(i))
+
+    @pl.loop(1, nz)
+    def _(i):
+        line_back_arrival(i).wait_recv()
+
+    for s in range(part):
+        for l in range(lane_tiles):
+            r = s * lane_tiles + l
+            acc[s : s + 1, l * LANES : (l + 1) * LANES] = z_all[r // per_z, r % per_z]
+    out_ref[chunk(core, xy)] = acc[...]
+
+    def plane_back_copy(i, g, device):
+        block = out_ref.at[chunk(core, g)]
+        return copy(block, block, send_sem.at[4], plane_back_sem.at[i - 1], device)
+
+    def pair_back_copy(i, which_core):
+        block = out_ref.at[chunk(which_core, behind(i))]
+        return copy(block, block, send_sem.at[5], pair_back_sem.at[i], sibling())
+
+    @pl.loop(1, planes)
+    def _(i):
+        plane_back_copy(i, xy, in_plane(ahead(i))).start()
+
+    pair_back_copy(0, core).start()
+
+    @pl.loop(1, planes)
+    def _(i):
+        plane_back_copy(i, behind(i), in_plane(ahead(i))).wait_recv()
+        pair_back_copy(i, core).start()
+
+    @pl.loop(0, planes)
+    def _(i):
+        pair_back_copy(i, 1 - core).wait_recv()
+
+    def drain(like, k):
+        pltpu.make_async_copy(like, like, send_sem.at[k]).wait()
+
+    drain(pair_buf, 0)
+    drain(plane_buf, 1)
+    drain(z_buf, 2)
+    drain(z_buf, 3)
+    drain(plane_buf, 4)
+    drain(pair_buf, 5)
+
+
+def all_sum(x, collective_id, nz, torus=TORUS):
+    nx, ny = torus
+    planes = nx * ny
+    rows, cols = x.shape
+    part = rows // (2 * planes)
+    per_z = part * cols // LANES // nz
+    dma = pltpu.SemaphoreType.DMA
+    return pl.pallas_call(
+        functools.partial(all_sum_kernel, nx, ny, nz),
+        out_shape=jax.ShapeDtypeStruct((rows, cols), jnp.float32),
+        in_specs=[pl.BlockSpec(memory_space=pltpu.VMEM)],
+        out_specs=pl.BlockSpec(memory_space=pltpu.VMEM),
+        scratch_shapes=[
+            pltpu.VMEM((rows // 2, cols), jnp.float32),
+            pltpu.VMEM((planes - 1, part, cols), jnp.float32),
+            pltpu.VMEM((part, cols), jnp.float32),
+            pltpu.VMEM((nz, per_z, 1, LANES), jnp.float32),
+            pltpu.VMEM((nz - 1, per_z, 1, LANES), jnp.float32),
+            pltpu.VMEM((nz, per_z, 1, LANES), jnp.float32),
+            dma((planes,)),
+            dma((planes - 1,)),
+            dma((nz - 1,)),
+            dma((nz - 1,)),
+            dma((planes - 1,)),
+            dma((planes,)),
+            dma((6,)),
+        ],
+        compiler_params=pltpu.CompilerParams(
+            collective_id=collective_id, has_side_effects=True, vmem_limit_bytes=40 << 20
+        ),
+        cost_estimate=pl.CostEstimate(
+            flops=2 * rows * cols, bytes_accessed=8 * rows * cols, transcendentals=0
+        ),
+    )(x)
+
+
+def split(value):
+    hi = value.astype(jnp.bfloat16)
+    return hi, (value - hi.astype(jnp.float32)).astype(jnp.bfloat16)
+
+
+def polar_kernel(cross_ref, out_ref, p_hi, p_lo, g_hi, g_lo):
+    width = cross_ref.shape[0]
+    tile = 256
+    cross = cross_ref[...]
+    total = jnp.sum(cross * cross, keepdims=True)
+    out_ref[...] = cross / (2.0 * jnp.sqrt((total + 1e-06) / width))
+
+    def times(a, b_hi, b_lo, dims):
+        dot = functools.partial(
+            lax.dot_general, dimension_numbers=(dims, ((), ())), preferred_element_type=jnp.float32
+        )
+        return dot(a[0], b_hi) + (dot(a[0], b_lo) + dot(a[1], b_hi))
+
+    @pl.loop(0, NS_STEPS)
+    def _(step):
+        hi, lo = split(out_ref[...])
+        p_hi[...] = hi
+        p_lo[...] = lo
+        for r in range(0, width, tile):
+            band = slice(r, r + tile)
+            gram = times((p_hi[band], p_lo[band]), p_hi[...], p_lo[...], ((1,), (1,)))
+            hi, lo = split(gram)
+            g_hi[band] = hi
+            g_lo[band] = lo
+        for r in range(0, width, tile):
+            band = slice(r, r + tile)
+            cubic = times((g_hi[band], g_lo[band]), p_hi[...], p_lo[...], ((1,), (0,)))
+            out_ref[band] = 1.5 * out_ref[band] - 0.5 * cubic
+
+
+def polar_factor(cross):
+    width = cross.shape[0]
+    return pl.pallas_call(
+        polar_kernel,
+        out_shape=jax.ShapeDtypeStruct((width, width), jnp.float32),
+        in_specs=[pl.BlockSpec(memory_space=pltpu.VMEM)],
+        out_specs=pl.BlockSpec(memory_space=pltpu.VMEM),
+        scratch_shapes=[pltpu.VMEM((width, width), jnp.bfloat16)] * 4,
+        compiler_params=pltpu.CompilerParams(vmem_limit_bytes=40 << 20),
+        cost_estimate=pl.CostEstimate(
+            flops=60 * width**3, bytes_accessed=8 * width * width, transcendentals=0
+        ),
+    )(cross)
 
 
 def onehot_rows(ids_group):
@@ -44,7 +303,12 @@
     groups = subspaces // 8
     grouped_ids = codeword_ids.reshape(rows_local, groups, 8).transpose(1, 0, 2)
     code_totals, code_counts = group_sums(embeddings, grouped_ids, sub_width, True)
-    code_totals, code_counts = lax.psum((code_totals, code_counts), ("grp", "dev"))
+    nz = lax.axis_size("dev")
+    summed = all_sum(
+        jnp.concatenate([code_totals.reshape(subspaces * sub_width, K),
+                         code_counts, jnp.zeros((160, K), jnp.float32)]), 1, nz)
+    code_totals = summed[:width].reshape(subspaces, sub_width, K)
+    code_counts = summed[width : width + subspaces]
     divisor = code_counts[:, None, :] + 1.0
     first_books = (code_totals / divisor).astype(jnp.bfloat16)
 
@@ -62,31 +326,14 @@
         embeddings, recon, (((0,), (0,)), ((), ())), preferred_element_type=jnp.float32
     )
     share = width // lax.axis_size("dev")
-    cross_full = lax.psum(partial_cross, ("grp", "dev"))
-    cross_own = lax.dynamic_slice_in_dim(cross_full, lax.axis_index("dev") * share, share, 0)
-    scale = 2.0 * jnp.sqrt((jnp.sum(cross_full * cross_full) + 1e-06) / width)
-    current_full = cross_full / scale
-    current_rows = cross_own / scale
-    for step_no in range(NS_STEPS):
-        if step_no > 0:
-            current_full = lax.all_gather(current_rows, "dev", axis=0, tiled=True)
-        inner = jnp.dot(
-            current_rows,
-            current_full.T,
-            precision=lax.Precision.HIGHEST,
-            preferred_element_type=jnp.float32,
-        )
-        cubic = jnp.dot(
-            inner, current_full, precision=lax.Precision.HIGHEST, preferred_element_type=jnp.float32
-        )
-        current_rows = 1.5 * current_rows - 0.5 * cubic
-    rotation_full = lax.all_gather(current_rows.astype(jnp.bfloat16), "dev", axis=0, tiled=True)
-    rotated = jnp.dot(embeddings, rotation_full, preferred_element_type=jnp.float32).astype(
-        jnp.bfloat16
-    )
+    rotation_full = polar_factor(all_sum(partial_cross, 2, nz))
+    own_rows = lax.dynamic_slice_in_dim(rotation_full, lax.axis_index("dev") * share, share, 0)
+    rotated = jnp.dot(
+        embeddings, rotation_full.astype(jnp.bfloat16), preferred_element_type=jnp.float32
+    ).astype(jnp.bfloat16)
     rotated_totals = group_sums(rotated, grouped_ids, sub_width, False)
-    rotated_totals = lax.psum(rotated_totals, ("grp", "dev"))
-    return (current_rows, rotated_totals / divisor)
+    rotated_totals = all_sum(rotated_totals.reshape(width, K), 3, nz)
+    return (own_rows, rotated_totals.reshape(subspaces, sub_width, K) / divisor)
 
 
 def solution(mesh):

time: 1910 us -> 277 us (0.15)
  waiting for transfers between devices: 1760 us -> 0 us
  Pallas kernels: 0 us -> 182 us
  matrix products: 78.5 us -> 51.6 us
    psum x3 -> x0, waiting for transfers between devices: 1420 us -> none  [the longest x1 477 us: on_device(): cross_full = lax.psum(partial_cross, ('grp', 'dev'))]
    all_gather x5 -> x0, waiting for transfers between devices: 345 us -> none  [the longest x4 277 us: on_device(): current_full = lax.all_gather(current_rows, 'dev', axis=0, tiled=True)]
    pallas_call x0 -> x4, Pallas kernels: none -> 182 us  [the longest x3 152 us: all_sum(): pl.pallas_call(functools.partial(all_sum_kernel, nx, ny, nz), out_shape=j...]
    dot_general x11 -> x1, matrix products: 31.9 us -> 1.71 us  [on_device(): jnp.dot(embeddings, rotation_full.astype(jnp.bfloat16), preferred_element...]
  transfers between devices with their start and end apart: 8 -> 0, of which waited for: 8 -> 0; matrix products, arithmetic and copies ran while one was open for 0% -> 0% of each run, Pallas kernels for 0% -> 0%
where the time goes in v1:
time: 277 us; the launch traced here: 273 us
  Pallas kernels  182 us (66%)
  matrix products  51.6 us (19%)
  local copies, waits for them, and re-layouts  28.6 us (10%)
  other arithmetic  10 us (4%)
    pallas_call x3, Pallas kernels, all_sum(): pl.pallas_call(functools.partial(all_sum_kernel, nx, ny, nz), out_shape=j...  152 us
    dot_general x24, matrix products, per_group(): jnp.einsum('rmj,rmk->mjk', values, selector, preferred_element_type=jnp.f...  37.2 us
    pallas_call x1, Pallas kernels, polar_factor(): pl.pallas_call(polar_kernel, out_shape=jax.ShapeDtypeStruct((width, width...  29.4 us
    eq x36, local copies, waits for them, and re-layouts, onehot_rows(): ids_group[:, :, None] == jnp.arange(K, dtype=jnp.int32)[None, None, :]  26.2 us
    dot_general x12, matrix products, rebuild(): jnp.einsum('rmk,mjk->rmj', selector, books_group, preferred_element_type=...  11.8 us
    reduce_sum x12, other arithmetic, per_group(): return (totals, jnp.sum(selector, axis=0, dtype=jnp.float32))  8.7 us

profile of v1, /device:TPU:1, one launch (start us, length us, event | category | flops | bytes accessed | tf_op | source)
XLA Modules:
  0.0 273.1 jit_solution(12291264983326535221)
XLA Ops:
  0.6 1.4 copy.4
  2.1 34.1 %while.32 = (s32[]{:T(128)}, f32[12,8,8,256]{3,2,1,0:T(8,128)S(1)}, f32[12,8,256]{2,1,0:T(8,128)S(1)}, bf16[12,512,64]{1,2,0:T(8,128)(2,1)S(1)}, s32[12,512,8]{1,2,0:T(8,128)}, /*index=5*/s32[]{:T(128)}) while((s32[]{:T(128)}, f32[12,8,8,256]{3,2,1,0:T(8,128)S(1)}, f32[12,8,256]{2,1,0:T(8,128)S(1)}, bf16[12,512,64]{1,2,0:T(8,128)(2,1)S(1)}, ...), condition=%wide.region_2.3_spmd, body=%wide.region_0.2_spmd.sunk | while | flops 22018048 | bytes 222293 | solution.py:293
  2.9 1.4 fusion.35
  5.7 1.4 fusion.35
  8.6 1.4 fusion.35
  11.4 1.4 fusion.35
  14.2 1.4 fusion.35
  17.1 1.4 fusion.35
  19.9 1.4 fusion.35
  22.8 1.4 fusion.35
  25.6 1.4 fusion.35
  28.5 1.4 fusion.35
  31.3 1.4 fusion.35
  34.2 1.4 fusion.35
  36.6 53.4 %shard_map.41 = f32[1024,256]{1,0:T(8,128)S(1)} custom-call(f32[1024,256]{1,0:T(8,128)S(1)} %maximum_maximum_fusion.x_ref), custom_call_target="tpu_custom_call" | custom-call | flops 524288 | bytes 2097152 | tf_op jit(solution)/shard_map/pallas_call | solution.py:190
  90.2 20.7 %while.33 = (s32[]{:T(128)}, bf16[12,512,64]{1,2,0:T(8,128)(2,1)S(1)}, bf16[12,8,8,256]{3,2,1,0:T(8,128)(2,1)S(1)}, s32[12,512,8]{1,2,0:T(8,128)}, s32[]{:T(128)}) while((s32[]{:T(128)}, bf16[12,512,64]{1,2,0:T(8,128)(2,1)S(1)}, bf16[12,8,8,256]{3,2,1,0:T(8,128)(2,1)S(1)}, s32[12,512,8]{1,2,0:T(8,128)}, s32[]{:T(128)}) %tuple.61), condition=%wide.region_4.5_spmd, body=%wide.region_3.4_spmd.sunk | while | flops 17858560 | bytes 148553 | solution.py:323
  90.2 0.8 dynamic-slice_bitcast_fusion.7
  91.0 1.0 fusion.37
  92.7 1.0 fusion.37
  94.5 1.0 fusion.37
  96.2 1.0 fusion.37
  97.9 1.0 fusion.37
  99.6 1.0 fusion.37
  101.3 1.0 fusion.37
  103.0 1.0 fusion.37
  104.8 1.0 fusion.37
  106.5 1.0 fusion.37
  108.2 1.0 fusion.37
  109.9 1.0 fusion.37
  110.9 0.8 convolution_bitcast_fusion.x_ref
  111.7 58.0 %shard_map.42.cross_ref = f32[768,768]{1,0:T(8,128)S(1)} custom-call(f32[768,768]{1,0:T(8,128)S(1)} %convolution_bitcast_fusion.x_ref), custom_call_target="tpu_custom_call" | custom-call | flops 1179648 | bytes 4718592 | tf_op jit(solution)/shard_map/pallas_call | solution.py:190
  169.8 29.4 %shard_map.43 = f32[768,768]{1,0:T(8,128)S(1)} custom-call(f32[768,768]{1,0:T(8,128)S(1)} %shard_map.42.cross_ref), custom_call_target="tpu_custom_call" | custom-call | flops 27179089920 | bytes 4718592 | tf_op jit(solution)/shard_map/pallas_call | solution.py:256
  199.8 1.7 convolution_convert_fusion
  201.6 29.6 %while.34 = (s32[]{:T(128)}, f32[12,8,8,256]{3,2,1,0:T(8,128)S(1)}, bf16[12,512,64]{1,2,0:T(8,128)(2,1)}, s32[12,512,8]{1,2,0:T(8,128)}, s32[]{:T(128)}) while((s32[]{:T(128)}, f32[12,8,8,256]{3,2,1,0:T(8,128)S(1)}, bf16[12,512,64]{1,2,0:T(8,128)(2,1)}, s32[12,512,8]{1,2,0:T(8,128)}, s32[]{:T(128)}) %tuple.62), condition=%wide.region_6.7_spmd, body=%wide.region_5.6_spmd.sunk | while | flops 17825792 | bytes 181321 | solution.py:293
  202.3 1.7 fusion.39
  204.8 1.7 fusion.39
  207.3 1.7 fusion.39
  209.7 1.7 fusion.39
  212.2 1.7 fusion.39
  214.7 1.7 fusion.39
  217.1 1.7 fusion.39
  219.6 1.7 fusion.39
  222.1 1.7 fusion.39
  224.5 1.7 fusion.39
  227.0 1.7 fusion.39
  229.5 1.7 fusion.39
  231.2 40.8 %shard_map.44 = f32[768,256]{1,0:T(8,128)S(1)} custom-call(f32[768,256]{1,0:T(8,128)S(1)} %bitcast.78), custom_call_target="tpu_custom_call" | custom-call | flops 393216 | bytes 1572864 | tf_op jit(solution)/shard_map/pallas_call | solution.py:190
  272.1 1.0 bitcast_divide_fusion
  (72 shorter events, 35.5 us)
Async XLA Ops:
  90.2 20.7 %copy-start = (bf16[512,768]{1,0:T(8,128)(2,1)S(1)}, bf16[512,768]{1,0:T(8,128)(2,1)}, u32[]{:S(2)}) copy-start(bf16[512,768]{1,0:T(8,128)(2,1)} %param.8) | copy-start | bytes 2359300

commit v2 on v0

v2 whole, which is shorter than its diff:
```python
import functools

import jax
import jax.numpy as jnp
from jax import lax
from jax.experimental import pallas as pl
from jax.experimental.pallas import tpu as pltpu
from jax.sharding import PartitionSpec as P

K = 256
NS_STEPS = 5
LANES = 128
MESH = pl.DeviceIdType.MESH
TORUS = (4, 4)
SUBW = 8
FIRST_CHUNKS = 4
CROSS_CHUNKS = 3
LAST_CHUNKS = 3
CHUNK = 256


class Place:
    def __init__(self, nx, ny, nz):
        self.nx, self.ny, self.nz, self.planes = nx, ny, nz, nx * ny
        self.grp, self.z = lax.axis_index("grp"), lax.axis_index("dev")
        self.core, self.xy = lax.rem(self.grp, 2), lax.div(self.grp, 2)
        self.x, self.y = lax.div(self.xy, ny), lax.rem(self.xy, ny)

    def sibling(self):
        return {"grp": self.xy * 2 + 1 - self.core, "dev": self.z}

    def plane_partner(self, i):
        nx, ny = self.nx, self.ny
        own = (nx - nx // 2) % nx * ny + (ny - ny // 2) % ny
        i = jnp.where(i >= own, i + 1, i)
        dx, dy = nx // 2 + lax.div(i, ny), ny // 2 + lax.rem(i, ny)
        return lax.rem(self.x + dx, nx) * ny + lax.rem(self.y + dy, ny)

    def in_plane(self, g):
        return {"grp": g * 2 + self.core, "dev": self.z}

    def line_partner(self, i):
        offset = self.nz // 2 + lax.div(i, 2) * (2 * lax.rem(i, 2) - 1)
        return lax.rem(self.z + offset, self.nz)

    def in_line(self, z):
        return {"grp": self.grp, "dev": z}

    def greet(self):
        barrier = pltpu.get_barrier_semaphore()

        def signal(device):
            pl.semaphore_signal(barrier, inc=1, device_id=device, device_id_type=MESH)

        signal(self.sibling())

        @pl.loop(0, self.planes - 1)
        def _(i):
            signal(self.in_plane(self.plane_partner(i)))

        @pl.loop(1, self.nz)
        def _(i):
            signal(self.in_line(self.line_partner(i)))

    def meet(self):
        pl.semaphore_wait(pltpu.get_barrier_semaphore(), 1 + self.planes - 1 + self.nz - 1)


def remote(src, dst, send, recv, device):
    return pltpu.make_async_remote_copy(
        src_ref=src, dst_ref=dst, send_sem=send, recv_sem=recv,
        device_id=device, device_id_type=MESH,
    )


def await_bytes(like, sem):
    pltpu.make_async_copy(like, like, sem).wait()


class AllSum:
    def __init__(self, place, refs):
        self.at = place
        (self.x, self.out, self.pair_buf, self.plane_buf, self.acc, self.z_src, self.z_buf,
         self.z_all, self.recv, self.send) = refs
        self.chunks, self.half, self.cols = self.pair_buf.shape
        self.part = self.half // place.planes
        self.lane_tiles = self.cols // LANES
        self.per_z = self.part * self.lane_tiles // place.nz

    def part_rows(self, c, core, g):
        return pl.ds(pl.multiple_of((2 * c + core) * self.half + g * self.part, 8), self.part)

    def half_rows(self, c, core):
        return pl.ds(pl.multiple_of((2 * c + core) * self.half, 8), self.half)

    def pair(self, c):
        at = self.at
        remote(
            self.x.at[self.half_rows(c, 1 - at.core)], self.pair_buf.at[c],
            self.send.at[0], self.recv.at[0, c], at.sibling(),
        ).start()

    def plane(self, c):
        at = self.at
        await_bytes(self.pair_buf.at[c], self.recv.at[0, c])
        self.pair_buf[c] = self.pair_buf[c] + self.x[self.half_rows(c, at.core)]

        @pl.loop(0, at.planes - 1)
        def _(i):
            g = at.plane_partner(i)
            rows = pl.ds(pl.multiple_of(g * self.part, 8), self.part)
            remote(
                self.pair_buf.at[c, rows], self.plane_buf.at[c, i],
                self.send.at[1], self.recv.at[1, c], at.in_plane(g),
            ).start()

    def line(self, c):
        at = self.at
        await_bytes(self.plane_buf.at[c], self.recv.at[1, c])
        rows = pl.ds(pl.multiple_of(at.xy * self.part, 8), self.part)
        total = self.pair_buf[c, rows]
        for i in range(at.planes - 1):
            total = total + self.plane_buf[c, i]
        self.acc[...] = total
        for s in range(self.part):
            for l in range(self.lane_tiles):
                r = s * self.lane_tiles + l
                self.z_src[c, r // self.per_z, r % self.per_z] = self.acc[
                    s : s + 1, l * LANES : (l + 1) * LANES
                ]

        @pl.loop(1, at.nz)
        def _(i):
            z = at.line_partner(i)
            remote(
                self.z_src.at[c, z], self.z_buf.at[c, i - 1],
                self.send.at[2], self.recv.at[2, c], at.in_line(z),
            ).start()

    def line_back(self, c):
        at = self.at
        await_bytes(self.z_buf.at[c], self.recv.at[2, c])
        total = self.z_src[c, at.z]
        for i in range(at.nz - 1):
            total = total + self.z_buf[c, i]
        self.z_all[c, at.z] = total

        @pl.loop(1, at.nz)
        def _(i):
            z = at.line_partner(i)
            block = self.z_all.at[c, at.z]
            remote(block, block, self.send.at[3], self.recv.at[3, c], at.in_line(z)).start()

    def plane_back(self, c):
        at = self.at
        await_bytes(self.z_buf.at[c], self.recv.at[3, c])
        for s in range(self.part):
            for l in range(self.lane_tiles):
                r = s * self.lane_tiles + l
                self.acc[s : s + 1, l * LANES : (l + 1) * LANES] = self.z_all[
                    c, r // self.per_z, r % self.per_z
                ]
        own = self.part_rows(c, at.core, at.xy)
        self.out[own] = self.acc[...]

        @pl.loop(0, at.planes - 1)
        def _(i):
            block = self.out.at[own]
            remote(
                block, block, self.send.at[4], self.recv.at[4, c],
                at.in_plane(at.plane_partner(i)),
            ).start()

    def pair_back(self, c):
        at = self.at
        await_bytes(self.plane_buf.at[c], self.recv.at[4, c])
        block = self.out.at[self.half_rows(c, at.core)]
        remote(block, block, self.send.at[5], self.recv.at[5, c], at.sibling()).start()

    def arrive(self, c):
        await_bytes(self.pair_buf.at[c], self.recv.at[5, c])

    def drain(self):
        for k, like in enumerate(
            (self.pair_buf, self.plane_buf, self.z_buf, self.z_buf, self.plane_buf, self.pair_buf)
        ):
            await_bytes(like, self.send.at[k])


def all_sum_scratch(chunks, rows, cols, nx, ny, nz):
    planes = nx * ny
    part = rows // (2 * planes)
    per_z = part * (cols // LANES) // nz
    return [
        pltpu.VMEM((chunks * rows, cols), jnp.float32),
        pltpu.VMEM((chunks * rows, cols), jnp.float32),
        pltpu.VMEM((chunks, rows // 2, cols), jnp.float32),
        pltpu.VMEM((chunks, planes - 1, part, cols), jnp.float32),
        pltpu.VMEM((part, cols), jnp.float32),
        pltpu.VMEM((chunks, nz, per_z, 1, LANES), jnp.float32),
        pltpu.VMEM((chunks, nz - 1, per_z, 1, LANES), jnp.float32),
        pltpu.VMEM((chunks, nz, per_z, 1, LANES), jnp.float32),
        pltpu.SemaphoreType.DMA((6, chunks)),
        pltpu.SemaphoreType.DMA((6,)),
    ]


def split(value):
    hi = value.astype(jnp.bfloat16)
    return hi, (value - hi.astype(jnp.float32)).astype(jnp.bfloat16)


def dot(a, b, dims):
    return lax.dot_general(
        a, b, dimension_numbers=(dims, ((), ())), preferred_element_type=jnp.float32
    )


def newton_schulz(cross, q, p_hi, p_lo, g_hi, g_lo):
    width = q.shape[0]
    tile = 256
    total = jnp.sum(cross[...] * cross[...], keepdims=True)
    q[...] = cross[...] / (2.0 * jnp.sqrt((total + 1e-06) / width))

    def times(a, b_hi, b_lo, dims):
        return dot(a[0], b_hi, dims) + (dot(a[0], b_lo, dims) + dot(a[1], b_hi, dims))

    @pl.loop(0, NS_STEPS)
    def _(step):
        hi, lo = split(q[...])
        p_hi[...] = hi
        p_lo[...] = lo
        for r in range(0, width, tile):
            band = slice(r, r + tile)
            gram = times((p_hi[band], p_lo[band]), p_hi[...], p_lo[...], ((1,), (1,)))
            hi, lo = split(gram)
            g_hi[band] = hi
            g_lo[band] = lo
        for r in range(0, width, tile):
            band = slice(r, r + tile)
            cubic = times((g_hi[band], g_lo[band]), p_hi[...], p_lo[...], ((1,), (0,)))
            q[band] = 1.5 * q[band] - 0.5 * cubic


def kernel(
    nx, ny, nz, emb, emb_t, ids_t, rot_out, books_out,
    *scratch,
):
    first_refs, cross_refs, last_refs = scratch[0:10], scratch[10:20], scratch[20:30]
    books, recon_t, counts, p_hi, p_lo, g_hi, g_lo, polar, rot, rot_t = scratch[30:]
    rows = emb.shape[0]
    width = emb.shape[1]
    place = Place(nx, ny, nz)
    place.greet()
    first = AllSum(place, first_refs)
    cross = AllSum(place, cross_refs)
    last = AllSum(place, last_refs)
    subs = 24
    top = lax.broadcasted_iota(jnp.int32, (2 * SUBW, rows), 0) < SUBW
    first_eight = lax.broadcasted_iota(jnp.int32, (2 * SUBW, K), 0) < SUBW
    codes = lax.broadcasted_iota(jnp.int32, (K, rows), 0).astype(jnp.float32).astype(jnp.bfloat16)
    one, zero = jnp.array(1, jnp.bfloat16), jnp.array(0, jnp.bfloat16)

    def selector(m):
        return jnp.where(ids_t[pl.ds(m, 1), :].astype(jnp.bfloat16) == codes, one, zero)

    def pair_rows(m):
        return pl.ds(pl.multiple_of(m * SUBW, 16), 2 * SUBW)

    def first_sums(t):
        base = t * CHUNK

        @pl.loop(0, subs // 8)
        def _(u):
            for s in range(0, 8, 2):
                m = u * 8 + s
                values = emb_t[pair_rows(t * subs + m), :]
                both = dot(jnp.where(top, values, one), selector(t * subs + m), ((1,), (1,)))
                at = pl.ds(pl.multiple_of(base + m * SUBW, 8), SUBW)
                first.x[at, :] = both[:SUBW]
                first.x[pl.ds(base + subs * SUBW + m, 1), :] = both[SUBW : SUBW + 1]
                both = dot(jnp.where(top, one, values), selector(t * subs + m + 1), ((1,), (1,)))
                at = pl.ds(pl.multiple_of(base + m * SUBW + SUBW, 8), SUBW)
                first.x[at, :] = both[SUBW:]
                first.x[pl.ds(base + subs * SUBW + m + 1, 1), :] = both[:1]

        used = subs * (SUBW + 1)
        first.x[base + used : base + CHUNK, :] = jnp.zeros((CHUNK - used, K), jnp.float32)

    def first_books(t):
        base = t * CHUNK
        tally = base + subs * SUBW
        counts[t * subs : (t + 1) * subs, :] = first.out[tally : tally + subs, :] + 1.0
        for m in range(0, subs, 2):
            g = t * subs + m
            divisor = jnp.where(first_eight, counts[g : g + 1, :], counts[g + 1 : g + 2, :])
            sums = first.out[base + m * SUBW : base + (m + 2) * SUBW, :]
            books[g * SUBW : (g + 2) * SUBW, :] = (sums / divisor).astype(jnp.bfloat16)

        @pl.loop(0, subs // 8)
        def _(u):
            for s in range(0, 8, 2):
                m = t * subs + u * 8 + s
                book = books[pair_rows(m), :]
                even = dot(book, selector(m), ((1,), (0,)))
                odd = dot(book, selector(m + 1), ((1,), (0,)))
                recon_t[pair_rows(m), :] = jnp.where(top, even, odd).astype(jnp.bfloat16)

    def cross_rows(j):
        band = slice(j * CHUNK, (j + 1) * CHUNK)
        cross.x[band, :] = dot(recon_t[band, :], emb[...], ((1,), (0,)))

    def last_sums(j):
        band = slice(j * CHUNK, (j + 1) * CHUNK)
        rot_t[...] = dot(p_hi[band, :], emb_t[...], ((1,), (0,))).astype(jnp.bfloat16)

        @pl.loop(0, CHUNK // SUBW // 8)
        def _(u):
            for s in range(0, 8, 2):
                m = u * 8 + s
                values = rot_t[pair_rows(m), :]
                base = j * CHUNK // SUBW
                even = dot(values, selector(base + m), ((1,), (1,)))
                odd = dot(values, selector(base + m + 1), ((1,), (1,)))
                at = pl.ds(pl.multiple_of(j * CHUNK + m * SUBW, 8), SUBW)
                last.x[at, :] = even[:SUBW]
                at = pl.ds(pl.multiple_of(j * CHUNK + m * SUBW + SUBW, 8), SUBW)
                last.x[at, :] = odd[SUBW:]

    first_sums(0)
    place.meet()
    first.pair(0)
    first_sums(1)
    first.pair(1)
    first.plane(0)
    first_sums(2)
    first.pair(2)
    first.plane(1)
    first_sums(3)
    first.pair(3)
    first.plane(2)
    first.line(0)
    first.plane(3)
    for t in range(1, FIRST_CHUNKS):
        first.line(t)
    for t in range(FIRST_CHUNKS):
        first.line_back(t)
    for t in range(FIRST_CHUNKS):
        first.plane_back(t)
    first.pair_back(0)
    first.pair_back(1)
    first.arrive(0)
    first_books(0)
    first.pair_back(2)
    first.arrive(1)
    first_books(1)
    cross_rows(0)
    cross.pair(0)
    first.pair_back(3)
    first.arrive(2)
    first_books(2)
    cross_rows(1)
    cross.pair(1)
    cross.plane(0)
    first.arrive(3)
    first_books(3)
    cross_rows(2)
    cross.pair(2)
    cross.plane(1)
    cross.line(0)
    cross.plane(2)
    cross.line(1)
    cross.line(2)
    for stage in (cross.line_back, cross.plane_back, cross.pair_back, cross.arrive):
        for t in range(CROSS_CHUNKS):
            stage(t)

    newton_schulz(cross.out, polar, p_hi, p_lo, g_hi, g_lo)
    p_hi[...] = polar[...].astype(jnp.bfloat16)
    last_sums(0)
    last.pair(0)
    last_sums(1)
    last.pair(1)
    last.plane(0)
    last_sums(2)
    last.pair(2)
    last.plane(1)
    last.line(0)
    last.plane(2)
    last.line(1)
    last.line(2)
    rot[...] = polar[...].T
    share = width // nz
    rot_out[...] = rot[pl.ds(pl.multiple_of(place.z * share, 8), share), :]
    for stage in (last.line_back, last.plane_back, last.pair_back):
        for t in range(LAST_CHUNKS):
            stage(t)
    for t in range(LAST_CHUNKS):
        last.arrive(t)
        for m in range(t * CHUNK // SUBW, (t + 1) * CHUNK // SUBW):
            at = slice(m * SUBW, (m + 1) * SUBW)
            books_out[at, :] = last.out[at, :] / counts[m : m + 1, :]
    first.drain()
    cross.drain()
    last.drain()


def on_device(nz, torus, embeddings, codeword_ids):
    nx, ny = torus
    rows, width = embeddings.shape
    vmem = pl.BlockSpec(memory_space=pltpu.VMEM)
    bf16 = jnp.bfloat16
    square = pltpu.VMEM((width, width), bf16)
    subspaces = codeword_ids.shape[1]
    rotation, books = pl.pallas_call(
        functools.partial(kernel, nx, ny, nz),
        out_shape=(
            jax.ShapeDtypeStruct((width // nz, width), jnp.float32),
            jax.ShapeDtypeStruct((width, K), jnp.float32),
        ),
        in_specs=[vmem] * 3,
        out_specs=(vmem, vmem),
        scratch_shapes=[
            *all_sum_scratch(FIRST_CHUNKS, CHUNK, K, nx, ny, nz),
            *all_sum_scratch(CROSS_CHUNKS, CHUNK, width, nx, ny, nz),
            *all_sum_scratch(LAST_CHUNKS, CHUNK, K, nx, ny, nz),
            pltpu.VMEM((width, K), bf16),
            pltpu.VMEM((width, rows), bf16),
            pltpu.VMEM((subspaces, K), jnp.float32),
            square, square, square, square,
            pltpu.VMEM((width, width), jnp.float32),
            pltpu.VMEM((width, width), jnp.float32),
            pltpu.VMEM((CHUNK, rows), bf16),
        ],
        compiler_params=pltpu.CompilerParams(
            collective_id=1, has_side_effects=True, vmem_limit_bytes=56 << 20
        ),
        cost_estimate=pl.CostEstimate(
            flops=60 * width**3, bytes_accessed=8 * width * width, transcendentals=0
        ),
    )(embeddings, embeddings.T, codeword_ids.T.astype(jnp.float32))
    return rotation, books.reshape(subspaces, SUBW, K)


def solution(mesh, torus=TORUS):
    return jax.shard_map(
        functools.partial(on_device, mesh.shape["dev"], torus),
        mesh=mesh,
        in_specs=(P(("grp", "dev"), None), P(("grp", "dev"), None)),
        out_specs=(P("dev", None), P()),
        check_vma=False,
    )
```

time: 1910 us -> 167 us (0.09)
  waiting for transfers between devices: 1760 us -> 0 us
  Pallas kernels: 0 us -> 159 us
  matrix products: 78.5 us -> 0 us
  local copies, waits for them, and re-layouts: 36.7 us -> 5.93 us
    psum x3 -> x0, waiting for transfers between devices: 1420 us -> none  [the longest x1 477 us: on_device(): cross_full = lax.psum(partial_cross, ('grp', 'dev'))]
    all_gather x5 -> x0, waiting for transfers between devices: 345 us -> none  [the longest x4 277 us: on_device(): current_full = lax.all_gather(current_rows, 'dev', axis=0, tiled=True)]
    pallas_call x0 -> x1, Pallas kernels: none -> 159 us  [on_device(): pl.pallas_call(functools.partial(kernel, nx, ny, nz), out_shape=(jax.Shap...]
    dot_general x48 -> x0, matrix products: 78.5 us -> none  [the longest x24 32.6 us: per_group(): jnp.einsum('rmj,rmk->mjk', values, selector, preferred_element_type=jnp.f...]
    eq x36 -> x0, local copies, waits for them, and re-layouts: 26.1 us -> none  [onehot_rows(): ids_group[:, :, None] == jnp.arange(K, dtype=jnp.int32)[None, None, :]]
  transfers between devices with their start and end apart: 8 -> 0, of which waited for: 8 -> 0; matrix products, arithmetic and copies ran while one was open for 0% -> 0% of each run, Pallas kernels for 0% -> 0%
where the time goes in v2:
time: 167 us
  Pallas kernels  159 us (95%)
  local copies, waits for them, and re-layouts  5.93 us (4%)
    pallas_call x1, Pallas kernels, on_device(): pl.pallas_call(functools.partial(kernel, nx, ny, nz), out_shape=(jax.Shap...  159 us
    unnamed x3, local copies, waits for them, and re-layouts  5.93 us

profile of v2, /device:TPU:1, one launch (start us, length us, event | category | flops | bytes accessed | tf_op | source)
XLA Modules:
  0.0 167.0 jit_solution(14522709681085907078)
XLA Ops:
  0.6 1.6 convert_bitcast_fusion.ids_t
  2.2 2.3 %copy.4 = bf16[512,768]{0,1:T(8,128)(2,1)} copy(bf16[512,768]{1,0:T(8,128)(2,1)} %emb.1) | data formatting | bytes 1572864 | tf_op args[0]
  4.5 158.8 %shard_map.41 = (f32[48,768]{1,0:T(8,128)}, f32[768,256]{1,0:T(8,128)}) custom-call(bf16[512,768]{1,0:T(8,128)(2,1)} %emb.1, bf16[768,512]{1,0:T(8,128)(2,1)} %bitcast.5, f32[96,512]{1,0:T(8,128)} %convert_bitcast_fusion.ids_t), custom_call_target="tpu_custom_call" | custom-call | flops 27179089920 | bytes 4718592 | tf_op jit(solution)/shard_map/pallas_call | solution.py:415
  163.3 1.6 copy.7
  164.9 2.1 %copy.8 = f32[96,8,256]{2,1,0:T(8,128)} copy(f32[96,8,256]{2,1,0:T(8,128)} %bitcast.4) | data formatting | bytes 1572864

commit v3 on v2

--- a/solution.py
+++ b/solution.py
@@ -19,12 +19,19 @@
 CHUNK = 256
 
 
+def line_shape(nz):
+    members = 4 if nz % 16 == 0 else nz // 2
+    return members, nz // members
+
+
 class Place:
     def __init__(self, nx, ny, nz):
         self.nx, self.ny, self.nz, self.planes = nx, ny, nz, nx * ny
         self.grp, self.z = lax.axis_index("grp"), lax.axis_index("dev")
         self.core, self.xy = lax.rem(self.grp, 2), lax.div(self.grp, 2)
         self.x, self.y = lax.div(self.xy, ny), lax.rem(self.xy, ny)
+        self.members, self.runs = line_shape(nz)
+        self.run, self.member = lax.div(self.z, self.members), lax.rem(self.z, self.members)
 
     def sibling(self):
         return {"grp": self.xy * 2 + 1 - self.core, "dev": self.z}
@@ -39,9 +46,17 @@
     def in_plane(self, g):
         return {"grp": g * 2 + self.core, "dev": self.z}
 
-    def line_partner(self, i):
-        offset = self.nz // 2 + lax.div(i, 2) * (2 * lax.rem(i, 2) - 1)
-        return lax.rem(self.z + offset, self.nz)
+    def member_partner(self, i):
+        return lax.rem(self.member + i, self.members)
+
+    def run_partner(self, i):
+        return lax.rem(self.run + i, self.runs)
+
+    def in_run(self, member):
+        return self.in_line(self.run * self.members + member)
+
+    def across_runs(self, run):
+        return self.in_line(run * self.members + self.member)
 
     def in_line(self, z):
         return {"grp": self.grp, "dev": z}
@@ -58,12 +73,14 @@
         def _(i):
             signal(self.in_plane(self.plane_partner(i)))
 
-        @pl.loop(1, self.nz)
-        def _(i):
-            signal(self.in_line(self.line_partner(i)))
+        for i in range(1, self.members):
+            signal(self.in_run(self.member_partner(i)))
+        for i in range(1, self.runs):
+            signal(self.across_runs(self.run_partner(i)))
 
     def meet(self):
-        pl.semaphore_wait(pltpu.get_barrier_semaphore(), 1 + self.planes - 1 + self.nz - 1)
+        partners = 1 + self.planes - 1 + self.members - 1 + self.runs - 1
+        pl.semaphore_wait(pltpu.get_barrier_semaphore(), partners)
 
 
 def remote(src, dst, send, recv, device):
@@ -81,11 +98,11 @@
     def __init__(self, place, refs):
         self.at = place
         (self.x, self.out, self.pair_buf, self.plane_buf, self.acc, self.z_src, self.z_buf,
-         self.z_all, self.recv, self.send) = refs
+         self.z_mid, self.z_all, self.recv, self.send) = refs
         self.chunks, self.half, self.cols = self.pair_buf.shape
         self.part = self.half // place.planes
         self.lane_tiles = self.cols // LANES
-        self.per_z = self.part * self.lane_tiles // place.nz
+        self.per_z = self.part * self.lane_tiles // place.members
 
     def part_rows(self, c, core, g):
         return pl.ds(pl.multiple_of((2 * c + core) * self.half + g * self.part, 8), self.part)
@@ -129,31 +146,44 @@
                     s : s + 1, l * LANES : (l + 1) * LANES
                 ]
 
-        @pl.loop(1, at.nz)
-        def _(i):
-            z = at.line_partner(i)
+        for i in range(1, at.members):
+            member = at.member_partner(i)
             remote(
-                self.z_src.at[c, z], self.z_buf.at[c, i - 1],
-                self.send.at[2], self.recv.at[2, c], at.in_line(z),
+                self.z_src.at[c, member], self.z_buf.at[c, i - 1],
+                self.send.at[2], self.recv.at[2, c], at.in_run(member),
             ).start()
 
+    def line_across(self, c):
+        at = self.at
+        await_bytes(self.z_buf.at[c], self.recv.at[2, c])
+        total = self.z_src[c, at.member]
+        for i in range(at.members - 1):
+            total = total + self.z_buf[c, i]
+        self.z_mid[c, at.run] = total
+        for i in range(1, at.runs):
+            block = self.z_mid.at[c, at.run]
+            remote(
+                block, block, self.send.at[3], self.recv.at[3, c],
+                at.across_runs(at.run_partner(i)),
+            ).start()
+
     def line_back(self, c):
         at = self.at
-        await_bytes(self.z_buf.at[c], self.recv.at[2, c])
-        total = self.z_src[c, at.z]
-        for i in range(at.nz - 1):
-            total = total + self.z_buf[c, i]
-        self.z_all[c, at.z] = total
-
-        @pl.loop(1, at.nz)
-        def _(i):
-            z = at.line_partner(i)
-            block = self.z_all.at[c, at.z]
-            remote(block, block, self.send.at[3], self.recv.at[3, c], at.in_line(z)).start()
+        await_bytes(self.z_mid.at[c, pl.ds(0, at.runs - 1)], self.recv.at[3, c])
+        total = self.z_mid[c, 0]
+        for i in range(1, at.runs):
+            total = total + self.z_mid[c, i]
+        self.z_all[c, at.member] = total
+        for i in range(1, at.members):
+            block = self.z_all.at[c, at.member]
+            remote(
+                block, block, self.send.at[6], self.recv.at[6, c],
+                at.in_run(at.member_partner(i)),
+            ).start()
 
     def plane_back(self, c):
         at = self.at
-        await_bytes(self.z_buf.at[c], self.recv.at[3, c])
+        await_bytes(self.z_buf.at[c], self.recv.at[6, c])
         for s in range(self.part):
             for l in range(self.lane_tiles):
                 r = s * self.lane_tiles + l
@@ -181,8 +211,10 @@
         await_bytes(self.pair_buf.at[c], self.recv.at[5, c])
 
     def drain(self):
+        across = self.z_mid.at[:, pl.ds(0, self.at.runs - 1)]
         for k, like in enumerate(
-            (self.pair_buf, self.plane_buf, self.z_buf, self.z_buf, self.plane_buf, self.pair_buf)
+            (self.pair_buf, self.plane_buf, self.z_buf, across, self.plane_buf, self.pair_buf,
+             self.z_buf)
         ):
             await_bytes(like, self.send.at[k])
 
@@ -190,18 +222,20 @@
 def all_sum_scratch(chunks, rows, cols, nx, ny, nz):
     planes = nx * ny
     part = rows // (2 * planes)
-    per_z = part * (cols // LANES) // nz
+    members, runs = line_shape(nz)
+    per_z = part * (cols // LANES) // members
     return [
         pltpu.VMEM((chunks * rows, cols), jnp.float32),
         pltpu.VMEM((chunks * rows, cols), jnp.float32),
         pltpu.VMEM((chunks, rows // 2, cols), jnp.float32),
         pltpu.VMEM((chunks, planes - 1, part, cols), jnp.float32),
         pltpu.VMEM((part, cols), jnp.float32),
-        pltpu.VMEM((chunks, nz, per_z, 1, LANES), jnp.float32),
-        pltpu.VMEM((chunks, nz - 1, per_z, 1, LANES), jnp.float32),
-        pltpu.VMEM((chunks, nz, per_z, 1, LANES), jnp.float32),
-        pltpu.SemaphoreType.DMA((6, chunks)),
-        pltpu.SemaphoreType.DMA((6,)),
+        pltpu.VMEM((chunks, members, per_z, 1, LANES), jnp.float32),
+        pltpu.VMEM((chunks, members - 1, per_z, 1, LANES), jnp.float32),
+        pltpu.VMEM((chunks, runs, per_z, 1, LANES), jnp.float32),
+        pltpu.VMEM((chunks, members, per_z, 1, LANES), jnp.float32),
+        pltpu.SemaphoreType.DMA((7, chunks)),
+        pltpu.SemaphoreType.DMA((7,)),
     ]
 
 
@@ -232,10 +266,12 @@
         p_lo[...] = lo
         for r in range(0, width, tile):
             band = slice(r, r + tile)
-            gram = times((p_hi[band], p_lo[band]), p_hi[...], p_lo[...], ((1,), (1,)))
-            hi, lo = split(gram)
-            g_hi[band] = hi
-            g_lo[band] = lo
+            for c in range(r, width, tile):
+                other = slice(c, c + tile)
+                gram = times((p_hi[band], p_lo[band]), p_hi[other], p_lo[other], ((1,), (1,)))
+                g_hi[band, other], g_lo[band, other] = split(gram)
+                if c > r:
+                    g_hi[other, band], g_lo[other, band] = split(gram.T)
         for r in range(0, width, tile):
             band = slice(r, r + tile)
             cubic = times((g_hi[band], g_lo[band]), p_hi[...], p_lo[...], ((1,), (0,)))
@@ -243,11 +279,12 @@
 
 
 def kernel(
-    nx, ny, nz, emb, emb_t, ids_t, rot_out, books_out,
+    nx, ny, nz, emb, ids_t, rot_out, last_out, counts,
     *scratch,
 ):
-    first_refs, cross_refs, last_refs = scratch[0:10], scratch[10:20], scratch[20:30]
-    books, recon_t, counts, p_hi, p_lo, g_hi, g_lo, polar, rot, rot_t = scratch[30:]
+    first_refs, cross_refs, last_refs = scratch[0:11], scratch[11:22], scratch[22:32]
+    last_refs = (last_refs[0], last_out, *last_refs[1:])
+    emb_t, books, recon_t, p_hi, p_lo, g_hi, g_lo, polar, rot, rot_t = scratch[32:]
     rows = emb.shape[0]
     width = emb.shape[1]
     place = Place(nx, ny, nz)
@@ -262,7 +299,7 @@
     one, zero = jnp.array(1, jnp.bfloat16), jnp.array(0, jnp.bfloat16)
 
     def selector(m):
-        return jnp.where(ids_t[pl.ds(m, 1), :].astype(jnp.bfloat16) == codes, one, zero)
+        return jnp.where(ids_t[pl.ds(m, 1), :].astype(jnp.float32).astype(jnp.bfloat16) == codes, one, zero)
 
     def pair_rows(m):
         return pl.ds(pl.multiple_of(m * SUBW, 16), 2 * SUBW)
@@ -270,10 +307,10 @@
     def first_sums(t):
         base = t * CHUNK
 
-        @pl.loop(0, subs // 8)
+        @pl.loop(0, 2)
         def _(u):
-            for s in range(0, 8, 2):
-                m = u * 8 + s
+            for s in range(0, subs // 2, 2):
+                m = u * (subs // 2) + s
                 values = emb_t[pair_rows(t * subs + m), :]
                 both = dot(jnp.where(top, values, one), selector(t * subs + m), ((1,), (1,)))
                 at = pl.ds(pl.multiple_of(base + m * SUBW, 8), SUBW)
@@ -314,10 +351,10 @@
         band = slice(j * CHUNK, (j + 1) * CHUNK)
         rot_t[...] = dot(p_hi[band, :], emb_t[...], ((1,), (0,))).astype(jnp.bfloat16)
 
-        @pl.loop(0, CHUNK // SUBW // 8)
+        @pl.loop(0, 2)
         def _(u):
-            for s in range(0, 8, 2):
-                m = u * 8 + s
+            for s in range(0, CHUNK // SUBW // 2, 2):
+                m = u * (CHUNK // SUBW // 2) + s
                 values = rot_t[pair_rows(m), :]
                 base = j * CHUNK // SUBW
                 even = dot(values, selector(base + m), ((1,), (1,)))
@@ -327,12 +364,19 @@
                 at = pl.ds(pl.multiple_of(j * CHUNK + m * SUBW + SUBW, 8), SUBW)
                 last.x[at, :] = odd[SUBW:]
 
+    def turn(t):
+        band = slice(t * CHUNK, (t + 1) * CHUNK)
+        emb_t[band, :] = emb[:, band].T
+
+    turn(0)
     first_sums(0)
+    turn(1)
     place.meet()
     first.pair(0)
     first_sums(1)
     first.pair(1)
     first.plane(0)
+    turn(2)
     first_sums(2)
     first.pair(2)
     first.plane(1)
@@ -343,6 +387,8 @@
     first.plane(3)
     for t in range(1, FIRST_CHUNKS):
         first.line(t)
+    for t in range(FIRST_CHUNKS):
+        first.line_across(t)
     for t in range(FIRST_CHUNKS):
         first.line_back(t)
     for t in range(FIRST_CHUNKS):
@@ -371,7 +417,7 @@
     cross.plane(2)
     cross.line(1)
     cross.line(2)
-    for stage in (cross.line_back, cross.plane_back, cross.pair_back, cross.arrive):
+    for stage in (cross.line_across, cross.line_back, cross.plane_back, cross.pair_back, cross.arrive):
         for t in range(CROSS_CHUNKS):
             stage(t)
 
@@ -392,17 +438,19 @@
     rot[...] = polar[...].T
     share = width // nz
     rot_out[...] = rot[pl.ds(pl.multiple_of(place.z * share, 8), share), :]
-    for stage in (last.line_back, last.plane_back, last.pair_back):
+    for stage in (last.line_across, last.line_back, last.plane_back, last.pair_back, last.arrive):
         for t in range(LAST_CHUNKS):
             stage(t)
-    for t in range(LAST_CHUNKS):
-        last.arrive(t)
-        for m in range(t * CHUNK // SUBW, (t + 1) * CHUNK // SUBW):
-            at = slice(m * SUBW, (m + 1) * SUBW)
-            books_out[at, :] = last.out[at, :] / counts[m : m + 1, :]
     first.drain()
     cross.drain()
     last.drain()
+
+
+def finish(sums, counts, rot, rot_out, books_out):
+    rot_out[...] = rot[...]
+    for m in range(counts.shape[0]):
+        at = slice(m * SUBW, (m + 1) * SUBW)
+        books_out[at, :] = sums[at, :] / counts[m : m + 1, :]
 
 
 def on_device(nz, torus, embeddings, codeword_ids):
@@ -412,33 +460,43 @@
     bf16 = jnp.bfloat16
     square = pltpu.VMEM((width, width), bf16)
     subspaces = codeword_ids.shape[1]
-    rotation, books = pl.pallas_call(
+    last_scratch = all_sum_scratch(LAST_CHUNKS, CHUNK, K, nx, ny, nz)
+    rotation_shape = jax.ShapeDtypeStruct((width // nz, width), jnp.float32)
+    books_shape = jax.ShapeDtypeStruct((width, K), jnp.float32)
+    rotation, sums, counts = pl.pallas_call(
         functools.partial(kernel, nx, ny, nz),
         out_shape=(
-            jax.ShapeDtypeStruct((width // nz, width), jnp.float32),
-            jax.ShapeDtypeStruct((width, K), jnp.float32),
+            rotation_shape, books_shape, jax.ShapeDtypeStruct((subspaces, K), jnp.float32),
         ),
-        in_specs=[vmem] * 3,
-        out_specs=(vmem, vmem),
+        in_specs=[vmem] * 2,
+        out_specs=(vmem, vmem, vmem),
         scratch_shapes=[
             *all_sum_scratch(FIRST_CHUNKS, CHUNK, K, nx, ny, nz),
             *all_sum_scratch(CROSS_CHUNKS, CHUNK, width, nx, ny, nz),
-            *all_sum_scratch(LAST_CHUNKS, CHUNK, K, nx, ny, nz),
+            last_scratch[0],
+            *last_scratch[2:],
+            pltpu.VMEM((width, rows), bf16),
             pltpu.VMEM((width, K), bf16),
             pltpu.VMEM((width, rows), bf16),
-            pltpu.VMEM((subspaces, K), jnp.float32),
             square, square, square, square,
             pltpu.VMEM((width, width), jnp.float32),
             pltpu.VMEM((width, width), jnp.float32),
             pltpu.VMEM((CHUNK, rows), bf16),
         ],
         compiler_params=pltpu.CompilerParams(
-            collective_id=1, has_side_effects=True, vmem_limit_bytes=56 << 20
+            collective_id=1, has_side_effects=True, vmem_limit_bytes=40 << 20
         ),
         cost_estimate=pl.CostEstimate(
             flops=60 * width**3, bytes_accessed=8 * width * width, transcendentals=0
         ),
-    )(embeddings, embeddings.T, codeword_ids.T.astype(jnp.float32))
+    )(embeddings, codeword_ids.T)
+    rotation, books = pl.pallas_call(
+        finish,
+        out_shape=(rotation_shape, books_shape),
+        in_specs=[vmem] * 3,
+        out_specs=(vmem, vmem),
+        compiler_params=pltpu.CompilerParams(vmem_limit_bytes=8 << 20),
+    )(sums, counts, rotation)
     return rotation, books.reshape(subspaces, SUBW, K)
 
 

time: 167 us -> 158 us (0.946)
  Pallas kernels: 159 us -> 155 us
  local copies, waits for them, and re-layouts: 5.93 us -> 2.05 us
    pallas_call x1 -> x2, Pallas kernels: 159 us -> 155 us  [the longest x1 154 us: on_device(): pl.pallas_call(functools.partial(kernel, nx, ny, nz), out_shape=(rotation...]
    unnamed x3 -> x4, local copies, waits for them, and re-layouts: 5.93 us -> 2.05 us
where the time goes in v3:
time: 158 us; the launch traced here: 157 us
  Pallas kernels  155 us (98%)
  local copies, waits for them, and re-layouts  2.05 us (1%)
    pallas_call x1, Pallas kernels, on_device(): pl.pallas_call(functools.partial(kernel, nx, ny, nz), out_shape=(rotation...  154 us

profile of v3, /device:TPU:1, one launch (start us, length us, event | category | flops | bytes accessed | tf_op | source)
XLA Modules:
  0.0 157.4 jit_solution(4500253950777691419)
XLA Ops:
  0.6 0.0 copy-start
  0.6 1.1 copy-done
  1.8 0.0 copy-start.1
  1.8 0.9 copy-done.1
  2.7 153.6 %shard_map.41 = (f32[48,768]{1,0:T(8,128)S(1)}, f32[768,256]{1,0:T(8,128)S(1)}, f32[96,256]{1,0:T(8,128)S(1)}) custom-call(bf16[512,768]{1,0:T(8,128)(2,1)S(1)} %copy-done, s32[96,512]{1,0:T(8,128)S(1)} %bitcast.2), custom_call_target="tpu_custom_call" | custom-call | flops 27179089920 | bytes 4718592 | tf_op jit(solution)/shard_map/pallas_call | solution.py:466
  156.3 1.0 shard_map.42
Async XLA Ops:
  0.6 1.1 copy-start
  1.8 0.9 copy-start.1

commit v4 on v3

--- a/solution.py
+++ b/solution.py
@@ -13,10 +13,12 @@
 MESH = pl.DeviceIdType.MESH
 TORUS = (4, 4)
 SUBW = 8
-FIRST_CHUNKS = 4
+FIRST_CHUNKS = 2
 CROSS_CHUNKS = 3
 LAST_CHUNKS = 3
 CHUNK = 256
+CHUNK_SUBS = 24
+BAND = 128
 
 
 def line_shape(nz):
@@ -97,45 +99,38 @@
 class AllSum:
     def __init__(self, place, refs):
         self.at = place
-        (self.x, self.out, self.pair_buf, self.plane_buf, self.acc, self.z_src, self.z_buf,
+        (self.x, self.out, self.plane_buf, self.acc, self.z_src, self.z_buf,
          self.z_mid, self.z_all, self.recv, self.send) = refs
-        self.chunks, self.half, self.cols = self.pair_buf.shape
-        self.part = self.half // place.planes
+        self.chunks, _, self.part, self.cols = self.plane_buf.shape
+        self.rows = self.part * place.planes
+        self.shared = self.out.shape[0] > self.x.shape[0]
         self.lane_tiles = self.cols // LANES
         self.per_z = self.part * self.lane_tiles // place.members
 
-    def part_rows(self, c, core, g):
-        return pl.ds(pl.multiple_of((2 * c + core) * self.half + g * self.part, 8), self.part)
-
-    def half_rows(self, c, core):
-        return pl.ds(pl.multiple_of((2 * c + core) * self.half, 8), self.half)
-
-    def pair(self, c):
-        at = self.at
-        remote(
-            self.x.at[self.half_rows(c, 1 - at.core)], self.pair_buf.at[c],
-            self.send.at[0], self.recv.at[0, c], at.sibling(),
-        ).start()
+    def out_rows(self, c, g, rows):
+        start = c * self.rows + g * self.part
+        if self.shared:
+            start = start + self.at.core * (self.chunks * self.rows)
+        return pl.ds(pl.multiple_of(start, 8), rows)
+
+    def x_rows(self, c, g):
+        return pl.ds(pl.multiple_of(c * self.rows + g * self.part, 8), self.part)
 
     def plane(self, c):
         at = self.at
-        await_bytes(self.pair_buf.at[c], self.recv.at[0, c])
-        self.pair_buf[c] = self.pair_buf[c] + self.x[self.half_rows(c, at.core)]
 
         @pl.loop(0, at.planes - 1)
         def _(i):
             g = at.plane_partner(i)
-            rows = pl.ds(pl.multiple_of(g * self.part, 8), self.part)
             remote(
-                self.pair_buf.at[c, rows], self.plane_buf.at[c, i],
+                self.x.at[self.x_rows(c, g)], self.plane_buf.at[c, i],
                 self.send.at[1], self.recv.at[1, c], at.in_plane(g),
             ).start()
 
     def line(self, c):
         at = self.at
         await_bytes(self.plane_buf.at[c], self.recv.at[1, c])
-        rows = pl.ds(pl.multiple_of(at.xy * self.part, 8), self.part)
-        total = self.pair_buf[c, rows]
+        total = self.x[self.x_rows(c, at.xy)]
         for i in range(at.planes - 1):
             total = total + self.plane_buf[c, i]
         self.acc[...] = total
@@ -190,7 +185,7 @@
                 self.acc[s : s + 1, l * LANES : (l + 1) * LANES] = self.z_all[
                     c, r // self.per_z, r % self.per_z
                 ]
-        own = self.part_rows(c, at.core, at.xy)
+        own = self.out_rows(c, at.xy, self.part)
         self.out[own] = self.acc[...]
 
         @pl.loop(0, at.planes - 1)
@@ -202,32 +197,31 @@
             ).start()
 
     def pair_back(self, c):
-        at = self.at
         await_bytes(self.plane_buf.at[c], self.recv.at[4, c])
-        block = self.out.at[self.half_rows(c, at.core)]
-        remote(block, block, self.send.at[5], self.recv.at[5, c], at.sibling()).start()
+        if self.shared:
+            block = self.out.at[self.out_rows(c, 0, self.rows)]
+            remote(block, block, self.send.at[5], self.recv.at[5, c], self.at.sibling()).start()
 
     def arrive(self, c):
-        await_bytes(self.pair_buf.at[c], self.recv.at[5, c])
+        await_bytes(self.x.at[pl.ds(c * self.rows, self.rows)], self.recv.at[5, c])
 
     def drain(self):
         across = self.z_mid.at[:, pl.ds(0, self.at.runs - 1)]
-        for k, like in enumerate(
-            (self.pair_buf, self.plane_buf, self.z_buf, across, self.plane_buf, self.pair_buf,
-             self.z_buf)
-        ):
+        waits = [(1, self.plane_buf), (2, self.z_buf), (3, across), (4, self.plane_buf), (6, self.z_buf)]
+        if self.shared:
+            waits.append((5, self.x))
+        for k, like in waits:
             await_bytes(like, self.send.at[k])
 
 
-def all_sum_scratch(chunks, rows, cols, nx, ny, nz):
+def all_sum_scratch(chunks, rows, cols, nx, ny, nz, shared):
     planes = nx * ny
-    part = rows // (2 * planes)
+    part = rows // planes
     members, runs = line_shape(nz)
     per_z = part * (cols // LANES) // members
     return [
         pltpu.VMEM((chunks * rows, cols), jnp.float32),
-        pltpu.VMEM((chunks * rows, cols), jnp.float32),
-        pltpu.VMEM((chunks, rows // 2, cols), jnp.float32),
+        pltpu.VMEM((chunks * rows * (2 if shared else 1), cols), jnp.float32),
         pltpu.VMEM((chunks, planes - 1, part, cols), jnp.float32),
         pltpu.VMEM((part, cols), jnp.float32),
         pltpu.VMEM((chunks, members, per_z, 1, LANES), jnp.float32),
@@ -282,165 +276,186 @@
     nx, ny, nz, emb, ids_t, rot_out, last_out, counts,
     *scratch,
 ):
-    first_refs, cross_refs, last_refs = scratch[0:11], scratch[11:22], scratch[22:32]
+    first_refs, cross_refs, last_refs = scratch[0:10], scratch[10:20], scratch[20:29]
     last_refs = (last_refs[0], last_out, *last_refs[1:])
-    emb_t, books, recon_t, p_hi, p_lo, g_hi, g_lo, polar, rot, rot_t = scratch[32:]
-    rows = emb.shape[0]
-    width = emb.shape[1]
+    (emb_all, emb_t, ids_all, books, recon_t, p_hi, p_lo, g_hi, g_lo, polar, rot, rot_t,
+     swap_recv, swap_send) = scratch[29:]
+    rows, width = emb.shape
+    half = width // 2
+    subs = half // SUBW
     place = Place(nx, ny, nz)
     place.greet()
     first = AllSum(place, first_refs)
     cross = AllSum(place, cross_refs)
     last = AllSum(place, last_refs)
-    subs = 24
-    top = lax.broadcasted_iota(jnp.int32, (2 * SUBW, rows), 0) < SUBW
+    both_rows = 2 * rows
+    bf16 = jnp.bfloat16
+    top = lax.broadcasted_iota(jnp.int32, (2 * SUBW, both_rows), 0) < SUBW
     first_eight = lax.broadcasted_iota(jnp.int32, (2 * SUBW, K), 0) < SUBW
-    codes = lax.broadcasted_iota(jnp.int32, (K, rows), 0).astype(jnp.float32).astype(jnp.bfloat16)
-    one, zero = jnp.array(1, jnp.bfloat16), jnp.array(0, jnp.bfloat16)
-
-    def selector(m):
-        return jnp.where(ids_t[pl.ds(m, 1), :].astype(jnp.float32).astype(jnp.bfloat16) == codes, one, zero)
+    codes = lax.broadcasted_iota(jnp.int32, (K, both_rows), 0).astype(jnp.float32).astype(bf16)
+    one, zero = jnp.array(1, bf16), jnp.array(0, bf16)
+    mine, other = slice(0, rows), slice(rows, both_rows)
+
+    def half_of(core, size):
+        return pl.ds(pl.multiple_of(core * size, size), size)
+
+    def selector(m, cols):
+        ids = ids_all[pl.ds(m, 1), cols].astype(jnp.float32).astype(bf16)
+        return jnp.where(ids == codes[:, cols], one, zero)
 
     def pair_rows(m):
         return pl.ds(pl.multiple_of(m * SUBW, 16), 2 * SUBW)
 
-    def first_sums(t):
+    def swaps():
+        core = place.core
+        theirs, ours = half_of(1 - core, half), half_of(core, half)
+        for k, (src, dst) in enumerate((
+            (ids_t.at[half_of(1 - core, subs), :], ids_all.at[:, other]),
+            (emb.at[:, theirs], emb_all.at[other, theirs]),
+            (emb.at[:, ours], emb_all.at[other, ours]),
+        )):
+            yield remote(src, dst, swap_send.at[k], swap_recv.at[k], place.sibling())
+
+    def landed(k, ref):
+        await_bytes(ref, swap_recv.at[k])
+
+    def first_sums(t, cols, part):
+        again = cols is other
         base = t * CHUNK
+        per = CHUNK_SUBS // 2
+
+        def put(at, value):
+            first.x[at, :] = first.x[at, :] + value if again else value
+
+        @pl.loop(part[0], part[1])
+        def _(u):
+            for s in range(0, per, 2):
+                m = u * per + s
+                values = emb_t[pair_rows(t * CHUNK_SUBS + m), cols]
+                even = dot(
+                    jnp.where(top[:, cols], values, one), selector(t * CHUNK_SUBS + m, cols), ((1,), (1,))
+                )
+                odd = dot(
+                    jnp.where(top[:, cols], one, values), selector(t * CHUNK_SUBS + m + 1, cols), ((1,), (1,))
+                )
+                put(pl.ds(pl.multiple_of(base + m * SUBW, 8), SUBW), even[:SUBW])
+                put(pl.ds(base + CHUNK_SUBS * SUBW + m, 1), even[SUBW : SUBW + 1])
+                put(pl.ds(pl.multiple_of(base + m * SUBW + SUBW, 8), SUBW), odd[SUBW:])
+                put(pl.ds(base + CHUNK_SUBS * SUBW + m + 1, 1), odd[:1])
+
+    def clear(t):
+        used = CHUNK_SUBS * (SUBW + 1)
+        first.x[t * CHUNK + used : (t + 1) * CHUNK, :] = jnp.zeros((CHUNK - used, K), jnp.float32)
+
+    def first_books(t):
+        base = t * CHUNK
+        tally = base + CHUNK_SUBS * SUBW
+        divisors = first.out[tally : tally + CHUNK_SUBS, :] + 1.0
+        own = pl.ds(pl.multiple_of(place.core * subs + t * CHUNK_SUBS, 8), CHUNK_SUBS)
+        counts[own, :] = divisors
+        for m in range(0, CHUNK_SUBS, 2):
+            g = t * CHUNK_SUBS + m
+            divisor = jnp.where(first_eight, divisors[m : m + 1, :], divisors[m + 1 : m + 2, :])
+            sums = first.out[base + m * SUBW : base + (m + 2) * SUBW, :]
+            books[g * SUBW : (g + 2) * SUBW, :] = (sums / divisor).astype(bf16)
+
+        @pl.loop(0, CHUNK_SUBS // 8)
+        def _(u):
+            for s in range(0, 8, 2):
+                m = t * CHUNK_SUBS + u * 8 + s
+                book = books[pair_rows(m), :]
+                even = dot(book, selector(m, slice(None)), ((1,), (0,)))
+                odd = dot(book, selector(m + 1, slice(None)), ((1,), (0,)))
+                recon_t[pair_rows(m), :] = jnp.where(top, even, odd).astype(bf16)
+
+    def counts_copy():
+        block = counts.at[half_of(place.core, subs), :]
+        return remote(block, block, swap_send.at[3], swap_recv.at[3], place.sibling())
+
+    def cross_rows(j):
+        band = slice(j * BAND, (j + 1) * BAND)
+        cross.x[band, :] = dot(recon_t[band, :], emb_all[...], ((1,), (0,)))
+
+    def last_sums(j):
+        own = pl.ds(pl.multiple_of(place.core * half + j * BAND, BAND), BAND)
+        rot_t[...] = dot(p_hi[own, :], emb_all[...], ((1,), (1,))).astype(bf16)
 
         @pl.loop(0, 2)
         def _(u):
-            for s in range(0, subs // 2, 2):
-                m = u * (subs // 2) + s
-                values = emb_t[pair_rows(t * subs + m), :]
-                both = dot(jnp.where(top, values, one), selector(t * subs + m), ((1,), (1,)))
-                at = pl.ds(pl.multiple_of(base + m * SUBW, 8), SUBW)
-                first.x[at, :] = both[:SUBW]
-                first.x[pl.ds(base + subs * SUBW + m, 1), :] = both[SUBW : SUBW + 1]
-                both = dot(jnp.where(top, one, values), selector(t * subs + m + 1), ((1,), (1,)))
-                at = pl.ds(pl.multiple_of(base + m * SUBW + SUBW, 8), SUBW)
-                first.x[at, :] = both[SUBW:]
-                first.x[pl.ds(base + subs * SUBW + m + 1, 1), :] = both[:1]
-
-        used = subs * (SUBW + 1)
-        first.x[base + used : base + CHUNK, :] = jnp.zeros((CHUNK - used, K), jnp.float32)
-
-    def first_books(t):
-        base = t * CHUNK
-        tally = base + subs * SUBW
-        counts[t * subs : (t + 1) * subs, :] = first.out[tally : tally + subs, :] + 1.0
-        for m in range(0, subs, 2):
-            g = t * subs + m
-            divisor = jnp.where(first_eight, counts[g : g + 1, :], counts[g + 1 : g + 2, :])
-            sums = first.out[base + m * SUBW : base + (m + 2) * SUBW, :]
-            books[g * SUBW : (g + 2) * SUBW, :] = (sums / divisor).astype(jnp.bfloat16)
-
-        @pl.loop(0, subs // 8)
-        def _(u):
-            for s in range(0, 8, 2):
-                m = t * subs + u * 8 + s
-                book = books[pair_rows(m), :]
-                even = dot(book, selector(m), ((1,), (0,)))
-                odd = dot(book, selector(m + 1), ((1,), (0,)))
-                recon_t[pair_rows(m), :] = jnp.where(top, even, odd).astype(jnp.bfloat16)
-
-    def cross_rows(j):
-        band = slice(j * CHUNK, (j + 1) * CHUNK)
-        cross.x[band, :] = dot(recon_t[band, :], emb[...], ((1,), (0,)))
-
-    def last_sums(j):
-        band = slice(j * CHUNK, (j + 1) * CHUNK)
-        rot_t[...] = dot(p_hi[band, :], emb_t[...], ((1,), (0,))).astype(jnp.bfloat16)
-
-        @pl.loop(0, 2)
-        def _(u):
-            for s in range(0, CHUNK // SUBW // 2, 2):
-                m = u * (CHUNK // SUBW // 2) + s
+            per = BAND // SUBW // 2
+            for s in range(0, per, 2):
+                m = u * per + s
                 values = rot_t[pair_rows(m), :]
-                base = j * CHUNK // SUBW
-                even = dot(values, selector(base + m), ((1,), (1,)))
-                odd = dot(values, selector(base + m + 1), ((1,), (1,)))
-                at = pl.ds(pl.multiple_of(j * CHUNK + m * SUBW, 8), SUBW)
+                base = j * BAND // SUBW
+                even = dot(values, selector(base + m, slice(None)), ((1,), (1,)))
+                odd = dot(values, selector(base + m + 1, slice(None)), ((1,), (1,)))
+                at = pl.ds(pl.multiple_of(j * BAND + m * SUBW, 8), SUBW)
                 last.x[at, :] = even[:SUBW]
-                at = pl.ds(pl.multiple_of(j * CHUNK + m * SUBW + SUBW, 8), SUBW)
+                at = pl.ds(pl.multiple_of(j * BAND + m * SUBW + SUBW, 8), SUBW)
                 last.x[at, :] = odd[SUBW:]
 
-    def turn(t):
-        band = slice(t * CHUNK, (t + 1) * CHUNK)
-        emb_t[band, :] = emb[:, band].T
-
-    turn(0)
-    first_sums(0)
-    turn(1)
+    ids_all[:, mine] = ids_t[half_of(place.core, subs), :]
+    emb_t[:, mine] = emb[:, half_of(place.core, half)].T
+    for t in range(FIRST_CHUNKS):
+        clear(t)
+    first_sums(0, mine, (0, 2))
+    first_sums(1, mine, (0, 1))
     place.meet()
-    first.pair(0)
-    first_sums(1)
-    first.pair(1)
+    for copy in swaps():
+        copy.start()
+    emb_all[mine, :] = emb[...]
+    first_sums(1, mine, (1, 2))
+    landed(0, ids_all.at[:, other])
+    landed(1, emb_all.at[other, pl.ds(0, half)])
+    emb_t[:, other] = emb_all[other, half_of(place.core, half)].T
+    first_sums(0, other, (0, 2))
     first.plane(0)
-    turn(2)
-    first_sums(2)
-    first.pair(2)
+    first_sums(1, other, (0, 2))
     first.plane(1)
-    first_sums(3)
-    first.pair(3)
-    first.plane(2)
-    first.line(0)
-    first.plane(3)
-    for t in range(1, FIRST_CHUNKS):
-        first.line(t)
-    for t in range(FIRST_CHUNKS):
-        first.line_across(t)
-    for t in range(FIRST_CHUNKS):
-        first.line_back(t)
-    for t in range(FIRST_CHUNKS):
-        first.plane_back(t)
+    landed(2, emb_all.at[other, pl.ds(0, half)])
+    stages = (first.line, first.line_across, first.line_back, first.plane_back)
+    for stage in stages:
+        for t in range(FIRST_CHUNKS):
+            stage(t)
     first.pair_back(0)
+    first_books(0)
+    cross_rows(0)
+    cross.plane(0)
     first.pair_back(1)
-    first.arrive(0)
-    first_books(0)
-    first.pair_back(2)
-    first.arrive(1)
     first_books(1)
-    cross_rows(0)
-    cross.pair(0)
-    first.pair_back(3)
-    first.arrive(2)
-    first_books(2)
     cross_rows(1)
-    cross.pair(1)
-    cross.plane(0)
-    first.arrive(3)
-    first_books(3)
+    cross.plane(1)
     cross_rows(2)
-    cross.pair(2)
-    cross.plane(1)
-    cross.line(0)
     cross.plane(2)
-    cross.line(1)
-    cross.line(2)
-    for stage in (cross.line_across, cross.line_back, cross.plane_back, cross.pair_back, cross.arrive):
+    counts_copy().start()
+    stages = (
+        cross.line, cross.line_across, cross.line_back, cross.plane_back, cross.pair_back,
+        cross.arrive,
+    )
+    for stage in stages:
         for t in range(CROSS_CHUNKS):
             stage(t)
 
     newton_schulz(cross.out, polar, p_hi, p_lo, g_hi, g_lo)
-    p_hi[...] = polar[...].astype(jnp.bfloat16)
+    p_hi[...] = polar[...].astype(bf16)
     last_sums(0)
-    last.pair(0)
+    last.plane(0)
     last_sums(1)
-    last.pair(1)
-    last.plane(0)
+    last.plane(1)
     last_sums(2)
-    last.pair(2)
-    last.plane(1)
-    last.line(0)
     last.plane(2)
-    last.line(1)
-    last.line(2)
+    for t in range(LAST_CHUNKS):
+        last.line(t)
     rot[...] = polar[...].T
     share = width // nz
     rot_out[...] = rot[pl.ds(pl.multiple_of(place.z * share, 8), share), :]
-    for stage in (last.line_across, last.line_back, last.plane_back, last.pair_back, last.arrive):
+    stages = (last.line_across, last.line_back, last.plane_back, last.pair_back, last.arrive)
+    for stage in stages:
         for t in range(LAST_CHUNKS):
             stage(t)
+    counts_copy().wait()
+    for copy in swaps():
+        copy.wait_send()
     first.drain()
     cross.drain()
     last.drain()
@@ -460,7 +475,8 @@
     bf16 = jnp.bfloat16
     square = pltpu.VMEM((width, width), bf16)
     subspaces = codeword_ids.shape[1]
-    last_scratch = all_sum_scratch(LAST_CHUNKS, CHUNK, K, nx, ny, nz)
+    last_scratch = all_sum_scratch(LAST_CHUNKS, BAND, K, nx, ny, nz, True)
+    half = width // 2
     rotation_shape = jax.ShapeDtypeStruct((width // nz, width), jnp.float32)
     books_shape = jax.ShapeDtypeStruct((width, K), jnp.float32)
     rotation, sums, counts = pl.pallas_call(
@@ -471,17 +487,21 @@
         in_specs=[vmem] * 2,
         out_specs=(vmem, vmem, vmem),
         scratch_shapes=[
-            *all_sum_scratch(FIRST_CHUNKS, CHUNK, K, nx, ny, nz),
-            *all_sum_scratch(CROSS_CHUNKS, CHUNK, width, nx, ny, nz),
+            *all_sum_scratch(FIRST_CHUNKS, CHUNK, K, nx, ny, nz, False),
+            *all_sum_scratch(CROSS_CHUNKS, BAND, width, nx, ny, nz, True),
             last_scratch[0],
             *last_scratch[2:],
-            pltpu.VMEM((width, rows), bf16),
-            pltpu.VMEM((width, K), bf16),
-            pltpu.VMEM((width, rows), bf16),
+            pltpu.VMEM((2 * rows, width), bf16),
+            pltpu.VMEM((half, 2 * rows), bf16),
+            pltpu.VMEM((subspaces // 2, 2 * rows), jnp.int32),
+            pltpu.VMEM((half, K), bf16),
+            pltpu.VMEM((half, 2 * rows), bf16),
             square, square, square, square,
             pltpu.VMEM((width, width), jnp.float32),
             pltpu.VMEM((width, width), jnp.float32),
-            pltpu.VMEM((CHUNK, rows), bf16),
+            pltpu.VMEM((BAND, 2 * rows), bf16),
+            pltpu.SemaphoreType.DMA((4,)),
+            pltpu.SemaphoreType.DMA((4,)),
         ],
         compiler_params=pltpu.CompilerParams(
             collective_id=1, has_side_effects=True, vmem_limit_bytes=40 << 20

time: 158 us -> 150 us (0.949)
  Pallas kernels: 155 us -> 147 us
    pallas_call x1, Pallas kernels: 154 us -> 146 us  [on_device(): pl.pallas_call(functools.partial(kernel, nx, ny, nz), out_shape=(rotation...]
where the time goes in v4:
time: 150 us
  Pallas kernels  147 us (98%)
  local copies, waits for them, and re-layouts  2.05 us (1%)
    pallas_call x1, Pallas kernels, on_device(): pl.pallas_call(functools.partial(kernel, nx, ny, nz), out_shape=(rotation...  146 us

profile of v4, /device:TPU:1, one launch (start us, length us, event | category | flops | bytes accessed | tf_op | source)
XLA Modules:
  0.0 149.7 jit_solution(8868244335960616873)
XLA Ops:
  0.6 0.0 copy-start
  0.6 1.1 copy-done
  1.8 0.0 copy-start.1
  1.8 0.9 copy-done.1
  2.7 145.9 %shard_map.41 = (f32[48,768]{1,0:T(8,128)S(1)}, f32[768,256]{1,0:T(8,128)S(1)}, f32[96,256]{1,0:T(8,128)S(1)}) custom-call(bf16[512,768]{1,0:T(8,128)(2,1)S(1)} %copy-done, s32[96,512]{1,0:T(8,128)S(1)} %bitcast.2), custom_call_target="tpu_custom_call" | custom-call | flops 27179089920 | bytes 4718592 | tf_op jit(solution)/shard_map/pallas_call | solution.py:482
  148.6 1.0 shard_map.42
Async XLA Ops:
  0.6 1.1 copy-start
  1.8 0.9 copy-start.1

commit v5 on v4

--- a/solution.py
+++ b/solution.py
@@ -248,28 +248,39 @@
     width = q.shape[0]
     tile = 256
     total = jnp.sum(cross[...] * cross[...], keepdims=True)
-    q[...] = cross[...] / (2.0 * jnp.sqrt((total + 1e-06) / width))
+    scale = 2.0 * jnp.sqrt((total + 1e-06) / width)
+    for r in range(0, width, tile):
+        band = slice(r, r + tile)
+        fresh = cross[band, :] / scale
+        q[band, :] = fresh
+        p_hi[0, band, :], p_lo[0, band, :] = split(fresh)
 
     def times(a, b_hi, b_lo, dims):
         return dot(a[0], b_hi, dims) + (dot(a[0], b_lo, dims) + dot(a[1], b_hi, dims))
 
-    @pl.loop(0, NS_STEPS)
-    def _(step):
-        hi, lo = split(q[...])
-        p_hi[...] = hi
-        p_lo[...] = lo
+    for step in range(NS_STEPS):
+        now = step % 2
+        hi, lo = p_hi.at[now], p_lo.at[now]
         for r in range(0, width, tile):
             band = slice(r, r + tile)
             for c in range(r, width, tile):
                 other = slice(c, c + tile)
-                gram = times((p_hi[band], p_lo[band]), p_hi[other], p_lo[other], ((1,), (1,)))
+                if c == r:
+                    mixed = dot(hi[band, :], lo[band, :], ((1,), (1,)))
+                    gram = dot(hi[band, :], hi[band, :], ((1,), (1,))) + (mixed + mixed.T)
+                else:
+                    gram = times(
+                        (hi[band, :], lo[band, :]), hi[other, :], lo[other, :], ((1,), (1,))
+                    )
                 g_hi[band, other], g_lo[band, other] = split(gram)
                 if c > r:
                     g_hi[other, band], g_lo[other, band] = split(gram.T)
         for r in range(0, width, tile):
             band = slice(r, r + tile)
-            cubic = times((g_hi[band], g_lo[band]), p_hi[...], p_lo[...], ((1,), (0,)))
-            q[band] = 1.5 * q[band] - 0.5 * cubic
+            cubic = times((g_hi[band, :], g_lo[band, :]), hi[...], lo[...], ((1,), (0,)))
+            fresh = 1.5 * q[band, :] - 0.5 * cubic
+            q[band, :] = fresh
+            p_hi[1 - now, band, :], p_lo[1 - now, band, :] = split(fresh)
 
 
 def kernel(
@@ -378,7 +389,7 @@
 
     def last_sums(j):
         own = pl.ds(pl.multiple_of(place.core * half + j * BAND, BAND), BAND)
-        rot_t[...] = dot(p_hi[own, :], emb_all[...], ((1,), (1,))).astype(bf16)
+        rot_t[...] = dot(p_hi[NS_STEPS % 2, own, :], emb_all[...], ((1,), (1,))).astype(bf16)
 
         @pl.loop(0, 2)
         def _(u):
@@ -437,7 +448,6 @@
             stage(t)
 
     newton_schulz(cross.out, polar, p_hi, p_lo, g_hi, g_lo)
-    p_hi[...] = polar[...].astype(bf16)
     last_sums(0)
     last.plane(0)
     last_sums(1)
@@ -496,7 +506,10 @@
             pltpu.VMEM((subspaces // 2, 2 * rows), jnp.int32),
             pltpu.VMEM((half, K), bf16),
             pltpu.VMEM((half, 2 * rows), bf16),
-            square, square, square, square,
+            pltpu.VMEM((2, width, width), bf16),
+            pltpu.VMEM((2, width, width), bf16),
+            square,
+            square,
             pltpu.VMEM((width, width), jnp.float32),
             pltpu.VMEM((width, width), jnp.float32),
             pltpu.VMEM((BAND, 2 * rows), bf16),

time: 150 us -> 147 us (0.980)
  Pallas kernels: 147 us -> 144 us
    pallas_call x1, Pallas kernels: 146 us -> 143 us  [on_device(): pl.pallas_call(functools.partial(kernel, nx, ny, nz), out_shape=(rotation...]
where the time goes in v5:
time: 147 us
  Pallas kernels  144 us (98%)
  local copies, waits for them, and re-layouts  2.05 us (1%)
    pallas_call x1, Pallas kernels, on_device(): pl.pallas_call(functools.partial(kernel, nx, ny, nz), out_shape=(rotation...  143 us

profile of v5, /device:TPU:1, one launch (start us, length us, event | category | flops | bytes accessed | tf_op | source)
XLA Modules:
  0.0 147.1 jit_solution(18017477001505411568)
XLA Ops:
  0.6 0.0 copy-start
  0.6 1.1 copy-done
  1.8 0.0 copy-start.1
  1.8 0.9 copy-done.1
  2.7 143.4 %shard_map.41 = (f32[48,768]{1,0:T(8,128)S(1)}, f32[768,256]{1,0:T(8,128)S(1)}, f32[96,256]{1,0:T(8,128)S(1)}) custom-call(bf16[512,768]{1,0:T(8,128)(2,1)S(1)} %copy-done, s32[96,512]{1,0:T(8,128)S(1)} %bitcast.2), custom_call_target="tpu_custom_call" | custom-call | flops 27179089920 | bytes 4718592 | tf_op jit(solution)/shard_map/pallas_call | solution.py:492
  146.1 1.0 shard_map.42
Async XLA Ops:
  0.6 1.1 copy-start
  1.8 0.9 copy-start.1
